TPU v7x, 32 devices: a whole 2x2x4 slice. The times are simulated.
32 devices in a mesh: wide: 8 (over z, core), narrow: 2 (over y), act: 2 (over x).
Axes of the slice: x: 2, y: 2, z: 4, core: 2. Of those that a mesh axis runs over, the one named last changes fastest.
Arguments:
- value_now: float32 [16, 16, 128, 128], P('wide', 'narrow'), may hold values from -8 to 8, as said below
- cost_first: float32 [8, 16], replicated, may hold values from -6 to 332, as said below
- cost_second: float32 [8, 16], replicated, may hold values from -6 to 6
- cost_third: float32 [8, 128], replicated, may hold values from -6 to 6
- cost_fourth: float32 [8, 128], replicated, may hold values from -6 to 6
- trans_weights: float32 [8, 4, 65], replicated, may hold values from 0.0001 to 1
- trans_offsets: int32 [8, 4], replicated, may hold values from -32 to 32
- action_order: int32 [8], replicated, may hold values from 0 to 7, each once
Outputs:
- new_value: float32 [16, 16, 128, 128], P('wide', 'narrow')
- choice_prob: bfloat16 [8, 16, 16, 128, 128], P('act', 'wide', 'narrow')
Inputs may be any that keep to these rules, and one draw needn't show every extreme that they name: `value_now`: A value function of order one with rough and broad variation. `cost_first`: flow utility terms of order one in most entries.
All inputs are finite; a program needn't handle non-finite values.
Results may differ from a plain program's by a relative error of at most 0.001.
Values sent between devices are 32-bit elements; how exact they have to be, the bound alone decides.
No kernel may reach another device: no remote copies, remote signals or barrier semaphores. Data moves between devices by JAX's collectives and lax.ppermute only.
A program may use at most 64 MiB of HBM per device.

v0:
```python
import functools

import jax
import jax.numpy as jnp
from jax import lax
from jax.experimental import pallas as pl
from jax.experimental.pallas import tpu as pltpu
from jax.sharding import PartitionSpec as P

DISCOUNT = 0.95
HIGHEST = lax.Precision.HIGHEST
F32 = jnp.float32
BF16 = jnp.bfloat16
LANES = 128
SUBLANES = 8
PLACE = 4
CHUNK_ROWS = 16
MIB = 1024 * 1024


def merged(value, axis, join):
    pieces = lax.all_gather(value, axis)
    head = pieces[0]
    tail = pieces[1:]
    subtotal, _ = lax.scan(lambda subtotal, slab: (join(subtotal, slab), None), head, tail)
    return subtotal


def transition(weights, offset, length):
    band_len = weights.shape[0]
    half_band = (band_len - 1) // 2
    normed = weights / jnp.sum(weights)
    row_ids = jnp.arange(length, dtype=jnp.int32)
    tap_ids = jnp.arange(band_len, dtype=jnp.int32)
    target = jnp.clip(row_ids[:, None] + offset + tap_ids[None, :] - half_band, 0, length - 1)
    matched = (target[:, :, None] == row_ids[None, None, :]).astype(normed.dtype)
    return jnp.einsum("ijk,j->ik", matched, normed, precision=HIGHEST)


def exchange_body(
    value_now,
    cost_first,
    cost_second,
    cost_third,
    cost_fourth,
    trans_weights,
    trans_offsets,
    action_order,
):
    size_act = lax.axis_size("act")
    per_group = action_order.shape[0] // size_act
    group_id = lax.axis_index("act")
    my_actions = lax.dynamic_slice_in_dim(action_order, group_id * per_group, per_group)
    rows_first, rows_second, len_third, len_fourth = value_now.shape
    len_first = rows_first * lax.axis_size("wide")
    len_second = rows_second * lax.axis_size("narrow")
    my_weights = jnp.take(trans_weights, my_actions, axis=0)
    my_offsets = jnp.take(trans_offsets, my_actions, axis=0)

    def build(axis_id, length):
        return jax.vmap(lambda weight_row, offset_one: transition(weight_row, offset_one, length))(
            my_weights[:, axis_id], my_offsets[:, axis_id]
        )

    mat_first = build(0, len_first)
    mat_second = build(1, len_second)
    mat_third = build(2, len_third)
    mat_fourth = build(3, len_fourth)
    spread = lax.all_to_all(value_now, "narrow", split_axis=2, concat_axis=1, tiled=True)
    field = jnp.einsum("gij,ajcd->gaicd", mat_second, spread, precision=HIGHEST)
    field = jnp.einsum("gij,gabcj->gabci", mat_fourth, field, precision=HIGHEST)
    field = lax.all_to_all(field, "narrow", split_axis=2, concat_axis=3, tiled=True)
    field = lax.all_to_all(field, "wide", split_axis=3, concat_axis=1, tiled=True)
    field = jnp.einsum("gij,gjbcd->gibcd", mat_first, field, precision=HIGHEST)
    field = lax.all_to_all(field, "wide", split_axis=1, concat_axis=3, tiled=True)
    expected = jnp.einsum("gij,gabjd->gabid", mat_third, field, precision=HIGHEST)
    start_first = lax.axis_index("wide") * rows_first
    start_second = lax.axis_index("narrow") * rows_second
    util_first = lax.dynamic_slice_in_dim(
        jnp.take(cost_first, my_actions, axis=0), start_first, rows_first, 1
    )
    util_second = lax.dynamic_slice_in_dim(
        jnp.take(cost_second, my_actions, axis=0), start_second, rows_second, 1
    )
    util_third = jnp.take(cost_third, my_actions, axis=0)
    util_fourth = jnp.take(cost_fourth, my_actions, axis=0)
    utility = (
        util_first[:, :, None, None, None]
        + util_second[:, None, :, None, None]
        + util_third[:, None, None, :, None]
        + util_fourth[:, None, None, None, :]
    )
    scores = utility + DISCOUNT * expected
    local_max = jnp.max(scores, axis=0)
    local_sum = jnp.sum(jnp.exp(scores - local_max), axis=0)
    log_total = merged(local_max + jnp.log(local_sum), "act", jnp.logaddexp)
    choice_prob = jnp.exp(scores - log_total).astype(jnp.bfloat16)
    return (log_total, choice_prob)


def halves(x):
    high = x.astype(BF16)
    return high, (x - high.astype(F32)).astype(BF16)


def dot32(a, b):
    return jnp.dot(a, b, preferred_element_type=F32, precision=HIGHEST)


def banded(weights, offset, length, taps):
    half_band = (taps - 1) // 2
    width = weights.shape[1]
    normed = weights / jnp.sum(weights, axis=1, keepdims=True)
    tile = jnp.broadcast_to(normed, (SUBLANES, width))
    tile = pltpu.roll(tile, lax.rem(offset + (width - half_band), width), 1)
    rows = jnp.concatenate([tile] * (length // SUBLANES), axis=0)
    rows = pltpu.roll(rows, 0, 1, stride=1, stride_axis=0)
    lane = lax.broadcasted_iota(jnp.int32, (length, width), 1)
    under = lane >= width - 2 * half_band
    over = (lane >= length) & (lane < length + 2 * half_band)
    under_sum = jnp.sum(jnp.where(under, rows, 0.0), axis=1, keepdims=True)
    over_sum = jnp.sum(jnp.where(over, rows, 0.0), axis=1, keepdims=True)
    span = -(-length // LANES) * LANES
    kept = lane[:, :span]
    body = jnp.where(kept < length, rows[:, :span], 0.0)
    body = body + jnp.where(kept == 0, under_sum, 0.0)
    return body + jnp.where(kept == length - 1, over_sum, 0.0)


def prepare_kernel(
    lengths, taps, sizes, rows0, rows1, arrivals, meta, weights,
    kron_hi, kron_lo, side_hi, side_lo, right3, wide0, wide1,
):
    n_act, n_narrow, n_outer = sizes
    len0, len1, len2, len3 = lengths
    act, narrow, outer, core = (meta[i] for i in range(PLACE))
    actions = weights.shape[0]
    per_group = actions // n_act
    columns = len0 * len1

    def wrapped(index, size):
        return lax.rem(index + size, size)

    lane = lax.broadcasted_iota(jnp.int32, (1, columns), 1)
    ids0 = jnp.zeros((1, columns), jnp.int32)
    ids1 = jnp.zeros((1, columns), jnp.int32)
    for block, (far, part, ahead) in enumerate(arrivals):
        from_outer, from_core = outer ^ far, wrapped(core + part, 2)
        for row in range(rows0):
            start = (block * rows0 + row) * rows1
            inside = (lane >= start) & (lane < start + rows1)
            first = (from_outer * 2 + from_core) * rows0 + row
            second = wrapped(narrow - ahead, n_narrow) * rows1 - start
            ids0 = jnp.where(inside, first, ids0)
            ids1 = jnp.where(inside, second + lane, ids1)
    spread0 = (lax.broadcasted_iota(jnp.int32, (LANES, columns), 0) == ids0).astype(F32)
    spread1 = (lax.broadcasted_iota(jnp.int32, (LANES, columns), 0) == ids1).astype(F32)

    for action in range(actions):
        group, slot = divmod(action, per_group)
        which = meta[PLACE + wrapped(act + group, n_act) * per_group + slot]
        rows = weights[which]
        mats = [
            banded(
                rows[axis : axis + 1, :],
                meta[PLACE + (1 + axis) * actions + which],
                lengths[axis],
                taps,
            )
            for axis in (0, 1, 3)
        ]
        wide0[...] = dot32(mats[0], spread0)
        wide1[...] = dot32(mats[1], spread1)
        base = (outer * 2 + core) * rows0
        products = []
        for ahead in range(n_narrow if group == 0 else 1):
            begin = wrapped(narrow + ahead, n_narrow) * rows1
            second = wide1[pl.ds(pl.multiple_of(begin, SUBLANES), rows1), :]
            blocks = [wide0[pl.ds(base + row, 1), :] * second for row in range(rows0)]
            high, low = halves(jnp.concatenate(blocks, axis=0))
            if ahead == 0:
                start = action * rows0 * rows1
                kron_hi[start : start + rows0 * rows1, :] = high
                kron_lo[start : start + rows0 * rows1, :] = low
            products.append(blocks)
        for row in range(rows0 if group == 0 else 0):
            high, low = halves(jnp.concatenate([blocks[row] for blocks in products], axis=0))
            start = (row * per_group + slot) * n_narrow * rows1
            side_hi[start : start + n_narrow * rows1, :] = high
            side_lo[start : start + n_narrow * rows1, :] = low
        high, low = halves(mats[2].T)
        row_pair = jnp.concatenate([high, low], axis=1)
        right3[action] = jnp.concatenate([row_pair, row_pair], axis=0)


def prepare_third_kernel(taps, segments, meta, weights, third, fourth, left2, util23):
    act, actions, per_group = meta[0], weights.shape[0], left2.shape[0]
    len2, len3 = util23.shape[1:]
    lane2 = lax.broadcasted_iota(jnp.int32, (1, len2), 1)
    ids2 = jnp.zeros((1, len2), jnp.int32)
    filled = 0
    for begin, size, axis, ahead, count in segments:
        source = begin + lax.rem(meta[axis] + ahead, count) * size
        inside = (lane2 >= filled) & (lane2 < filled + size)
        ids2 = jnp.where(inside, source - filled + lane2, ids2)
        filled += size
    order2 = (lax.broadcasted_iota(jnp.int32, (len2, len2), 0) == ids2).astype(F32)

    for slot in range(per_group):
        which = meta[PLACE + act * per_group + slot]
        offset = meta[PLACE + 3 * actions + which]
        matrix = banded(weights[which][2:3, :], offset, len2, taps)
        high, low = halves(dot32(matrix, order2))
        left2[slot] = jnp.concatenate(
            [jnp.concatenate([high, high], axis=1), jnp.concatenate([low, low], axis=1)], axis=0
        )
        column = jnp.broadcast_to(third[pl.ds(which, 1), :], (len3, len2)).T
        util23[slot] = column + fourth[pl.ds(which, 1), :]


def short_dims_kernel(views, routes, kron_hi, kron_lo, right3, *refs):
    n_inputs = 1 + max(view[0] for view in views)
    inputs, outs = refs[:n_inputs], refs[n_inputs:]
    rows, depth = outs[0].shape[2:]
    per_action = kron_hi.shape[0] // len(routes)
    q_hi, q_lo = kron_hi[...], kron_lo[...]
    mixed = []
    for row in range(0, rows, 2):
        cols = [
            jnp.concatenate(
                [
                    inputs[which][lead : lead + count, start + row + extra, :]
                    for which, lead, count, start in views
                ],
                axis=0,
            )
            for extra in range(2)
        ]
        x_hi, x_lo = halves(jnp.concatenate(cols, axis=1))
        out = (
            jnp.dot(q_hi, x_hi, preferred_element_type=F32)
            + jnp.dot(q_hi, x_lo, preferred_element_type=F32)
            + jnp.dot(q_lo, x_hi, preferred_element_type=F32)
        )
        mixed += [out[:, :depth], out[:, depth:]]
    for action, route in enumerate(routes):
        start = action * per_action
        block = jnp.concatenate([one[start : start + per_action] for one in mixed], axis=0)
        t_hi, t_lo = halves(block)
        both = jnp.dot(
            jnp.concatenate([t_hi, t_lo], axis=1), right3[action], preferred_element_type=F32
        )
        done = both[:, :depth] + both[:, depth:]
        for row in range(rows):
            first = row * per_action
            for which, slot in route:
                count = outs[which].shape[1]
                outs[which][slot, :, row, :] = done[first : first + count]
                first += count


def third_dim_kernel(n_pieces, rows0, row, meta, costs0, costs1, left2, util23, *refs):
    pieces, scores, local = refs[:n_pieces], refs[n_pieces], refs[n_pieces + 1]
    per_group, rows1 = scores.shape[:2]
    length = util23.shape[1]
    depth = util23.shape[2]
    which = [meta[PLACE + meta[0] * per_group + slot] for slot in range(per_group)]
    first = (meta[2] * 2 + meta[3]) * rows0 + row
    start1 = meta[1] * rows1
    for second in range(0, rows1, 2):
        for slot in range(per_group):
            cols = [
                jnp.concatenate([piece[slot, second + extra] for piece in pieces], axis=0)
                for extra in range(2)
            ]
            g_hi, g_lo = halves(jnp.concatenate(cols, axis=1))
            both = jnp.dot(
                left2[slot], jnp.concatenate([g_hi, g_lo], axis=0), preferred_element_type=F32
            )
            expected = both[:length] + both[length:]
            for extra in range(2):
                flat = costs0[which[slot], first] + costs1[which[slot], start1 + second + extra]
                scores[slot, second + extra] = (util23[slot] + flat) + DISCOUNT * expected[
                    :, extra * depth : (extra + 1) * depth
                ]
        for extra in range(2):
            found = [scores[slot, second + extra] for slot in range(per_group)]
            top = functools.reduce(jnp.maximum, found)
            total = functools.reduce(jnp.add, [jnp.exp(one - top) for one in found])
            local[second + extra] = top + jnp.log(total)


def choice_kernel(scores, mine, other, *refs):
    new_value, choice_prob = refs[-2:]
    a, b = mine[...], other[...]
    top, low = jnp.maximum(a, b), jnp.minimum(a, b)
    total = top + jnp.log(1.0 + jnp.exp(low - top))
    new_value[0] = total
    for slot in range(scores.shape[0]):
        choice_prob[slot, 0] = jnp.exp(scores[slot] - total).astype(choice_prob.dtype)


def after(value, *done):
    return lax.optimization_barrier((value, *done))[0] if done else value


def whole_block():
    return pl.BlockSpec(memory_space=pltpu.VMEM)


def params(mebibytes):
    return pltpu.CompilerParams(vmem_limit_bytes=mebibytes * MIB)


def gather_body(
    value_now,
    cost_first,
    cost_second,
    cost_third,
    cost_fourth,
    trans_weights,
    trans_offsets,
    action_order,
):
    n_act, n_narrow, n_wide = (lax.axis_size(name) for name in ("act", "narrow", "wide"))
    n_outer = n_wide // 2
    act, narrow, wide = (lax.axis_index(name) for name in ("act", "narrow", "wide"))
    outer, core = wide // 2, wide % 2
    actions, _, taps = trans_weights.shape
    per_group = actions // n_act
    rows0, rows1, len2, len3 = value_now.shape
    len0, len1 = rows0 * n_wide, rows1 * n_narrow
    lengths = (len0, len1, len2, len3)
    chunk = CHUNK_ROWS
    share = (len2 - n_narrow * chunk) // n_act
    n_chunks = share // chunk
    core_flip = [(i, i ^ 1) for i in range(n_wide)]
    act_flip = [(i, (i + 1) % n_act) for i in range(n_act)]
    narrow_flip = [(i, (i + 1) % n_narrow) for i in range(n_narrow)]

    def across(bit):
        return [(i, i ^ (2 * bit)) for i in range(n_wide)]

    def part(begin, size):
        return lax.dynamic_slice_in_dim(value_now, begin, size, 2)

    near = [(0, other, ahead) for ahead in range(n_narrow) for other in range(2)]
    arrivals = near + [
        (far, other, ahead)
        for ahead in range(n_narrow)
        for other in range(2)
        for far in range(1, n_outer)
    ]

    half_band = (taps - 1) // 2
    width = -(-(max(lengths) + 4 * half_band) // LANES) * LANES
    weights = jnp.pad(trans_weights, ((0, 0), (0, 0), (0, width - taps)))
    place = jnp.stack([act, narrow, outer, core]).astype(jnp.int32)
    meta = jnp.concatenate([place, action_order, trans_offsets.T.reshape(-1)])
    smem = pl.BlockSpec(memory_space=pltpu.SMEM)
    q_rows = actions * rows0 * rows1
    kron_hi, kron_lo, side_hi, side_lo, right3 = pl.pallas_call(
        functools.partial(
            prepare_kernel, lengths, taps, (n_act, n_narrow, n_outer), rows0, rows1, arrivals
        ),
        out_shape=(
            jax.ShapeDtypeStruct((q_rows, len0 * len1), BF16),
            jax.ShapeDtypeStruct((q_rows, len0 * len1), BF16),
            jax.ShapeDtypeStruct((q_rows * n_narrow // n_act, len0 * len1), BF16),
            jax.ShapeDtypeStruct((q_rows * n_narrow // n_act, len0 * len1), BF16),
            jax.ShapeDtypeStruct((actions, 2 * len3, 2 * len3), BF16),
        ),
        in_specs=[smem, whole_block()],
        out_specs=(whole_block(),) * 5,
        scratch_shapes=[pltpu.VMEM((len0, len0 * len1), F32), pltpu.VMEM((len1, len0 * len1), F32)],
        compiler_params=params(16),
        cost_estimate=pl.CostEstimate(flops=10**9, bytes_accessed=4 * 10**6, transcendentals=0),
        name="prepare",
    )(meta, weights)
    segments = [(0, share, 0, ahead, n_act) for ahead in range(n_act)]
    segments += [(n_act * share, chunk, 1, ahead, n_narrow) for ahead in range(n_narrow)]
    left2, util23 = pl.pallas_call(
        functools.partial(prepare_third_kernel, taps, segments),
        out_shape=(
            jax.ShapeDtypeStruct((per_group, 2 * len2, 2 * len2), BF16),
            jax.ShapeDtypeStruct((per_group, len2, len3), F32),
        ),
        in_specs=[smem] + [whole_block()] * 3,
        out_specs=(whole_block(),) * 2,
        compiler_params=params(12),
        cost_estimate=pl.CostEstimate(flops=10**9, bytes_accessed=4 * 10**6, transcendentals=0),
        name="prepare_third",
    )(meta, weights, cost_third, cost_fourth)

    side_begin = n_act * share
    inner = (outer == 1) | (outer == 2)
    value_now, inner, place, act_begin, own_begin, other_begin = lax.optimization_barrier(
        (
            value_now,
            inner,
            place,
            act * share,
            side_begin + narrow * chunk,
            side_begin + (n_narrow - 1 - narrow) * chunk,
        )
    )
    chunks = [part(act_begin + index * chunk, chunk) for index in range(n_chunks)]
    to_narrow = jnp.concatenate([part(act_begin, share), part(other_begin, chunk)], axis=2)
    own_side = part(own_begin, chunk)
    mine = jnp.concatenate([part(act_begin, share), own_side], axis=2)
    direct = [lax.ppermute(chunks[0], "wide", across(far)) for far in range(1, n_outer)]
    around = lax.ppermute(to_narrow, "narrow", narrow_flip)
    soon = lax.ppermute(part(act_begin + chunk, share - chunk), "wide", across(1))
    direct, *_ = lax.optimization_barrier((direct, kron_hi, right3))
    side = jnp.concatenate([own_side, around[:, :, share:]], axis=0)

    bits = [1 << bit for bit in range(1, n_outer.bit_length() - 1)]

    def doubled(own, twin, *done):
        size = own.shape[0]
        blocks = [own, twin]
        for bit in bits:
            grown = after(jnp.concatenate(blocks, axis=0), *done)
            more = lax.ppermute(grown, "wide", across(bit))
            blocks += [more[i : i + size] for i in range(0, more.shape[0], size)]
        return blocks[1:]

    inner_swap = [(2 * a + c, 2 * b + c) for a, b in ((1, 2), (2, 1)) for c in range(2)]
    outward = [(2 * a + c, 2 * b + c) for a, b in ((1, 0), (2, 3)) for c in range(2)]

    def by_line(own, twin, *done):
        size = own.shape[0]
        grown = after(jnp.concatenate([own, twin], axis=0), *done)
        came = lax.ppermute(grown, "wide", inner_swap)
        passed = lax.ppermute(after(came, moved[-1]), "wide", outward)
        return [
            twin,
            jnp.where(inner, came[size:], passed[:size]),
            jnp.where(inner, came[:size], passed[size:]),
        ]

    far0 = jnp.concatenate(direct, axis=0)
    crossed = [lax.ppermute(far0, "wide", core_flip)]
    moved = [lax.ppermute(far0, "narrow", narrow_flip)]
    late = lax.ppermute(after(side, far0), "wide", across(1))
    owns = chunks + [side]
    twins = [None] + [soon[:, :, i : i + chunk] for i in range(0, share - chunk, chunk)] + [late]
    nears = [mine, lax.ppermute(after(mine, crossed[0]), "wide", core_flip)]
    nears += [around, lax.ppermute(after(around, crossed[0]), "wide", core_flip)]
    nears = [one.reshape(rows0 * rows1, share + chunk, len3) for one in nears]

    def contract(kron, views, routes, out_rows, inputs):
        return pl.pallas_call(
            functools.partial(short_dims_kernel, views, routes),
            out_shape=tuple(
                jax.ShapeDtypeStruct((per_group, rows, chunk, len3), F32) for rows in out_rows
            ),
            in_specs=[whole_block()] * (3 + len(inputs)),
            out_specs=(whole_block(),) * len(out_rows),
            compiler_params=params(12),
            cost_estimate=pl.CostEstimate(flops=10**6, bytes_accessed=10**4, transcendentals=0),
            name="short_dims",
        )(*kron, right3, *inputs)

    block_rows = rows0 * rows1
    far_rows = (n_outer - 1) * block_rows
    def halved(one):
        return [one[i : i + rows0] for i in range(0, n_narrow * rows0, rows0)]

    side_early = [lax.ppermute(half, "wide", core_flip) for half in halved(late)]
    fars = [far0]
    kept, sent = [], []
    for index in range(n_chunks):
        far = fars[index]
        if index:
            if index == 1:
                far = after(far, late)
            crossed.append(lax.ppermute(far, "wide", core_flip))
            moved.append(lax.ppermute(after(far, moved[-1]), "narrow", narrow_flip))
        spread = by_line if index + 1 == n_chunks and n_outer == 4 else doubled
        done = [fars[index]] + ([], moved[:1], kept[:1] + moved[1:2])[min(index, 2)]
        blocks = spread(owns[index + 1], twins[index + 1], *done)
        fars.append(jnp.concatenate(blocks, axis=0))
        ready = ([left2, util23], side_early, ())[min(index, 2)]
        handed = lax.ppermute(after(moved[index], *ready), "wide", core_flip)
        pieces = [far, crossed[index], moved[index], handed]
        inputs = nears + [one.reshape(far_rows, chunk, len3) for one in pieces]
        views = [(i, 0, block_rows, index * chunk) for i in range(len(nears))]
        views += [(len(nears) + i, 0, far_rows, 0) for i in range(len(pieces))]
        cuts = rows0 if index == n_chunks - 1 else 1
        routes = [[(0, slot)] for slot in range(per_group)]
        routes += [[(1 + cut, slot) for cut in range(cuts)] for slot in range(per_group)]
        out_rows = [block_rows] + [block_rows // cuts] * cuts
        keep, *for_act = contract((kron_hi, kron_lo), views, routes, out_rows, inputs)
        kept.append(keep)
        sent.append([])
        for one in for_act:
            before = [one for ones in sent for one in ones][-1:]
            sent[-1].append(lax.ppermute(after(one, *before), "act", act_flip))

    turned = side_early + [
        lax.ppermute(half, "wide", core_flip) for one in blocks[1:] for half in halved(one)
    ]
    inputs = nears + [one.reshape(-1, chunk, len3) for one in blocks + turned]
    views = [(i, 0, block_rows, share) for i in range(len(nears))]
    for ahead in range(n_narrow):
        views += [(len(nears) + i, ahead * block_rows, block_rows, 0) for i in range(len(blocks))]
        first = len(nears) + len(blocks) + ahead
        views += [(first + n_narrow * i, 0, block_rows, 0) for i in range(len(blocks))]
    routes = [[(0, slot), (1, slot)] for slot in range(per_group)]
    count = side_hi.shape[0] // rows0
    ready = sent[-1][:1]
    side_keep, side_got = [], []
    for row in range(rows0):
        kron = [one[row * count : (row + 1) * count] for one in (side_hi, side_lo)]
        kron[0] = after(kron[0], *ready)
        keep, give = contract(kron, views, routes, [rows1, rows1], inputs)
        side_keep.append(keep)
        side_got.append(lax.ppermute(after(give, *side_got[-1:]), "narrow", narrow_flip))
        ready = [give]

    parts = [(keep, None) for keep in kept] + [(ones[0], None) for ones in sent[:-1]]
    parts += [(sent[-1][0], sent[-1]), (side_keep[0], side_keep), (side_got[0], side_got)]
    by_row = []
    for row in range(rows0):
        arrays = [cut[row] if cut else one for one, cut in parts]
        specs = [
            pl.BlockSpec(
                (per_group, rows1) + one.shape[2:],
                lambda i, block=0 if cut else row: (0, block, 0, 0),
            )
            for one, (_, cut) in zip(arrays, parts)
        ]
        scores, local = pl.pallas_call(
            functools.partial(third_dim_kernel, len(parts), rows0, row),
            grid=(1,),
            out_shape=(
                jax.ShapeDtypeStruct((per_group, rows1, len2, len3), F32),
                jax.ShapeDtypeStruct((rows1, len2, len3), F32),
            ),
            in_specs=[smem] * 3 + [whole_block()] * 2 + specs,
            out_specs=(whole_block(),) * 2,
            compiler_params=params(20),
            cost_estimate=pl.CostEstimate(
                flops=10**9, bytes_accessed=5 * 10**6, transcendentals=10**6
            ),
            name="third_dim",
        )(meta, cost_first, cost_second, left2, util23, *arrays)
        by_row.append((scores, local, lax.ppermute(local, "act", act_flip)))

    results = ()
    for row, operands in enumerate(by_row):
        results = pl.pallas_call(
            choice_kernel,
            grid=(1,),
            out_shape=(
                jax.ShapeDtypeStruct(value_now.shape, F32),
                jax.ShapeDtypeStruct((per_group,) + value_now.shape, BF16),
            ),
            in_specs=[whole_block()] * 3 + [pl.BlockSpec(memory_space=pl.ANY)] * len(results),
            out_specs=(
                pl.BlockSpec((1, rows1, len2, len3), lambda i, row=row: (row, 0, 0, 0)),
                pl.BlockSpec(
                    (per_group, 1, rows1, len2, len3), lambda i, row=row: (0, row, 0, 0, 0)
                ),
            ),
            input_output_aliases={3: 0, 4: 1} if results else {},
            compiler_params=params(16),
            cost_estimate=pl.CostEstimate(
                flops=10**7, bytes_accessed=5 * 10**6, transcendentals=10**6
            ),
            name="choice",
        )(*operands, *results)
    return tuple(results)


def gather_fits(mesh, value_shape, actions, offset_reach):
    n_wide, n_narrow, n_act = (mesh.shape[name] for name in ("wide", "narrow", "act"))
    len0, len1, len2, len3 = value_shape
    if n_act != 2 or n_wide < 4 or n_wide & (n_wide - 1) or actions % n_act:
        return False
    if n_narrow != 2 or len2 % (n_act * CHUNK_ROWS) or len2 < 4 * n_act * CHUNK_ROWS:
        return False
    if len2 != LANES or len3 != LANES:
        return False
    if (len1 // n_narrow) % SUBLANES or len0 * len1 // (n_wide * n_narrow) % 16 or len0 % n_wide:
        return False
    if max(len0, len1) > LANES or len1 % n_narrow:
        return False
    raw = len0 * len1 * len2 * len3 // (2 * n_act)
    exchanged = 2 * (actions // n_act) * len0 * len1 * len2 * len3 // (n_wide * n_narrow)
    return raw <= exchanged


def solution(mesh):
    def run(value_now, *rest):
        actions = rest[-1].shape[0]
        small = gather_fits(mesh, value_now.shape, actions, rest[4].shape[-1])
        return jax.shard_map(
            gather_body if small else exchange_body,
            mesh=mesh,
            in_specs=(P("wide", "narrow", None, None), P(), P(), P(), P(), P(), P(), P()),
            out_specs=(P("wide", "narrow", None, None), P("act", "wide", "narrow", None, None)),
            check_vma=False,
        )(value_now, *rest)

    return run
```

profile of v0, /device:TPU:0, one launch (start us, length us, event | category | flops | bytes accessed | tf_op | source)
XLA Modules:
  0.0 118.7 jit_solution(7741914998227879787)
XLA Ops:
  2.0 3.1 %collective-permute-start = (f32[2,8,16,128]{3,2,1,0:T(8,128)S(1)}, f32[2,8,16,128]{3,2,1,0:T(8,128)S(1)}, u32[]{:S(2)}, u32[]{:S(2)}) collective-permute-start(f32[2,8,16,128]{3,2,1,0:T(8,128)S(1)} %get-tuple-element.107), channel_id=1, source_target_pairs={{0,8},{4,12},{8,0},{12,4},{16,24},{20,28},{24,16},{28,20},{1,9},{5... | collective-permute-start | bytes 393224 | tf_op jit(solution)/shard_map/ppermute | solution.py:411
  5.1 2.6 %collective-permute-start.1 = (f32[2,8,16,128]{3,2,1,0:T(8,128)S(1)}, f32[2,8,16,128]{3,2,1,0:T(8,128)S(1)}, u32[]{:S(2)}, u32[]{:S(2)}) collective-permute-start(f32[2,8,16,128]{3,2,1,0:T(8,128)S(1)} %get-tuple-element.107), channel_id=1, source_target_pairs={{0,16},{4,20},{8,24},{12,28},{16,0},{20,4},{24,8},{28,12},{1,17},{... | collective-permute-start | bytes 393224 | tf_op jit(solution)/shard_map/ppermute | solution.py:411
  8.9 1.8 %collective-permute-start.5 = (f32[2,8,64,128]{3,2,1,0:T(8,128)S(1)}, f32[2,8,64,128]{3,2,1,0:T(8,128)S(1)}, u32[]{:S(2)}, u32[]{:S(2)}) collective-permute-start(f32[2,8,64,128]{3,2,1,0:T(8,128)S(1)} %get-tuple-element.109), channel_id=1, source_target_pairs={{0,2},{2,0},{1,3},{3,1},{4,6},{6,4},{5,7},{7,5},{8,10},{10,8},{9,1... | collective-permute-start | bytes 1572872 | tf_op jit(solution)/shard_map/ppermute | solution.py:412
  12.6 4.7 %prepare.1 = (bf16[128,256]{1,0:T(8,128)(2,1)S(1)}, bf16[128,256]{1,0:T(8,128)(2,1)S(1)}, bf16[128,256]{1,0:T(8,128)(2,1)S(1)}, bf16[128,256]{1,0:T(8,128)(2,1)S(1)}, bf16[8,256,256]{2,1,0:T(8,128)(2,1)S(1)}) custom-call(s32[44]{0:T(128)S(1)} %concatenate.34.meta, f32[8,4,256]{2,1,0:T(4,128)S(1)} %pad.4.weights), custom_call_target="tpu_custom_call" | custom-call | flops 1000000000 | bytes 4000000 | tf_op jit(solution)/shard_map/prepare/pallas_call | solution.py:362
  18.2 1.6 %collective-permute-start.7 = (f32[6,8,16,128]{3,2,1,0:T(8,128)S(1)}, f32[6,8,16,128]{3,2,1,0:T(8,128)S(1)}, u32[]{:S(2)}, u32[]{:S(2)}) collective-permute-start(f32[6,8,16,128]{3,2,1,0:T(8,128)S(1)} %constant_dynamic-update-slice_fusion), channel_id=1, source_target_pairs={{0,2},{2,0},{1,3},{3,1},{4,6},{6,4},{5,7},{7,5},{8,10},{10,8},{9,1... | collective-permute-start | bytes 1179656 | tf_op jit(solution)/shard_map/ppermute | solution.py:444
  19.8 2.3 %collective-permute-done.9 = f32[2,8,32,128]{3,2,1,0:T(8,128)S(1)} collective-permute-done((f32[2,8,32,128]{3,2,1,0:T(8,128)S(1)}, f32[2,8,32,128]{3,2,1,0:T(8,128)S(1)}, u32[]{:S(2)}, u32[]{:S(2)}) %collective-permute-start.9) | collective-permute-done | bytes 262176 | tf_op jit(solution)/shard_map/ppermute | solution.py:413
  23.0 2.5 %collective-permute-start.11 = (f32[4,8,16,128]{3,2,1,0:T(8,128)S(1)}, f32[4,8,16,128]{3,2,1,0:T(8,128)S(1)}, u32[]{:S(2)}, u32[]{:S(2)}) collective-permute-start(f32[4,8,16,128]{3,2,1,0:T(8,128)S(1)} %pad_maximum_fusion.6), channel_id=1, source_target_pairs={{0,8},{4,12},{8,0},{12,4},{16,24},{20,28},{24,16},{28,20},{1,9},{5... | collective-permute-start | bytes 786440 | tf_op jit(solution)/shard_map/ppermute | solution.py:445
  27.5 3.0 %collective-permute-done.7 = f32[6,8,16,128]{3,2,1,0:T(8,128)S(1)} collective-permute-done((f32[6,8,16,128]{3,2,1,0:T(8,128)S(1)}, f32[6,8,16,128]{3,2,1,0:T(8,128)S(1)}, u32[]{:S(2)}, u32[]{:S(2)}) %collective-permute-start.7) | collective-permute-done | bytes 393248 | tf_op jit(solution)/shard_map/ppermute | solution.py:444
  30.5 5.6 %collective-permute-done.10 = f32[4,8,16,128]{3,2,1,0:T(8,128)S(1)} collective-permute-done((f32[4,8,16,128]{3,2,1,0:T(8,128)S(1)}, f32[4,8,16,128]{3,2,1,0:T(8,128)S(1)}, u32[]{:S(2)}, u32[]{:S(2)}) %collective-permute-start.10) | collective-permute-done | bytes 262176 | tf_op jit(solution)/shard_map/ppermute | solution.py:424
  37.4 2.3 %short_dims.5 = (f32[4,16,16,128]{3,2,1,0:T(8,128)S(1)}, f32[4,16,16,128]{3,2,1,0:T(8,128)S(1)}) custom-call(bf16[128,256]{1,0:T(8,128)(2,1)S(1)} %get-tuple-element.54.kron_hi, bf16[128,256]{1,0:T(8,128)(2,1)S(1)} %get-tuple-element.55.kron_lo, bf16[8,256,256]{2,1,0:T(8,128)(2,1)S(1)} %get-tuple-element.56.right3, f32[16,64,128]{2,1,0:T(8,128)S(1)} %bitcast.30, ...), custom_call_target="tpu_custom_call" | custom-call | flops 1000000 | bytes 10000 | tf_op jit(solution)/shard_map/short_dims/pallas_call | solution.py:453
  39.7 1.5 %collective-permute-start.21 = (f32[4,16,16,128]{3,2,1,0:T(8,128)S(1)}, f32[4,16,16,128]{3,2,1,0:T(8,128)S(1)}, u32[]{:S(2)}, u32[]{:S(2)}) collective-permute-start(f32[4,16,16,128]{3,2,1,0:T(8,128)S(1)} %get-tuple-element.77), channel_id=1, source_target_pairs={{0,1},{1,0},{2,3},{3,2},{4,5},{5,4},{6,7},{7,6},{8,9},{9,8},{10,11... | collective-permute-start | bytes 1572872 | tf_op jit(solution)/shard_map/ppermute | solution.py:499
  41.2 9.1 %collective-permute-done.17 = f32[4,8,16,128]{3,2,1,0:T(8,128)S(1)} collective-permute-done((f32[4,8,16,128]{3,2,1,0:T(8,128)S(1)}, f32[4,8,16,128]{3,2,1,0:T(8,128)S(1)}, u32[]{:S(2)}, u32[]{:S(2)}) %collective-permute-start.17) | collective-permute-done | bytes 262176 | tf_op jit(solution)/shard_map/ppermute | solution.py:424
  53.3 2.3 %short_dims.6 = (f32[4,16,16,128]{3,2,1,0:T(8,128)S(1)}, f32[4,16,16,128]{3,2,1,0:T(8,128)S(1)}) custom-call(bf16[128,256]{1,0:T(8,128)(2,1)S(1)} %get-tuple-element.54.kron_hi, bf16[128,256]{1,0:T(8,128)(2,1)S(1)} %get-tuple-element.55.kron_lo, bf16[8,256,256]{2,1,0:T(8,128)(2,1)S(1)} %get-tuple-element.56.right3, f32[16,64,128]{2,1,0:T(8,128)S(1)} %bitcast.31, ...), custom_call_target="tpu_custom_call" | custom-call | flops 1000000 | bytes 10000 | tf_op jit(solution)/shard_map/short_dims/pallas_call | solution.py:453
  55.6 1.6 %collective-permute-start.22 = (f32[4,16,16,128]{3,2,1,0:T(8,128)S(1)}, f32[4,16,16,128]{3,2,1,0:T(8,128)S(1)}, u32[]{:S(2)}, u32[]{:S(2)}) collective-permute-start(f32[4,16,16,128]{3,2,1,0:T(8,128)S(1)} %get-tuple-element.79), channel_id=1, source_target_pairs={{0,1},{1,0},{2,3},{3,2},{4,5},{5,4},{6,7},{7,6},{8,9},{9,8},{10,11... | collective-permute-start | bytes 1572872 | tf_op jit(solution)/shard_map/ppermute | solution.py:499
  57.2 5.5 %collective-permute-done.19 = f32[6,8,16,128]{3,2,1,0:T(8,128)S(1)} collective-permute-done((f32[6,8,16,128]{3,2,1,0:T(8,128)S(1)}, f32[6,8,16,128]{3,2,1,0:T(8,128)S(1)}, u32[]{:S(2)}, u32[]{:S(2)}) %collective-permute-start.19) | collective-permute-done | bytes 393248 | tf_op jit(solution)/shard_map/ppermute | solution.py:479
  62.7 1.5 %collective-permute-start.26 = (f32[8,8,16,128]{3,2,1,0:T(8,128)S(1)}, f32[8,8,16,128]{3,2,1,0:T(8,128)S(1)}, u32[]{:S(2)}, u32[]{:S(2)}) collective-permute-start(f32[8,8,16,128]{3,2,1,0:T(8,128)S(1)} %collective-permute-done.25), channel_id=1, source_target_pairs={{8,0},{12,4},{16,24},{20,28},{9,1},{13,5},{17,25},{21,29},{10,2},{... | collective-permute-start | bytes 1572872 | tf_op jit(solution)/shard_map/ppermute | solution.py:435
  66.5 2.3 %short_dims.7 = (f32[4,16,16,128]{3,2,1,0:T(8,128)S(1)}, f32[4,8,16,128]{3,2,1,0:T(8,128)S(1)}, f32[4,8,16,128]{3,2,1,0:T(8,128)S(1)}) custom-call(bf16[128,256]{1,0:T(8,128)(2,1)S(1)} %get-tuple-element.54.kron_hi, bf16[128,256]{1,0:T(8,128)(2,1)S(1)} %get-tuple-element.55.kron_lo, bf16[8,256,256]{2,1,0:T(8,128)(2,1)S(1)} %get-tuple-element.56.right3, ...), custom_call_target="tpu_custom_call" | custom-call | flops 1000000 | bytes 10000 | tf_op jit(solution)/shard_map/short_dims/pallas_call | solution.py:453
  69.7 1.5 %collective-permute-start.23 = (f32[4,8,16,128]{3,2,1,0:T(8,128)S(1)}, f32[4,8,16,128]{3,2,1,0:T(8,128)S(1)}, u32[]{:S(2)}, u32[]{:S(2)}) collective-permute-start(f32[4,8,16,128]{3,2,1,0:T(8,128)S(1)} %get-tuple-element.82), channel_id=1, source_target_pairs={{0,1},{1,0},{2,3},{3,2},{4,5},{5,4},{6,7},{7,6},{8,9},{9,8},{10,11... | collective-permute-start | bytes 786440 | tf_op jit(solution)/shard_map/ppermute | solution.py:499
  71.2 6.5 %collective-permute-done.26 = f32[8,8,16,128]{3,2,1,0:T(8,128)S(1)} collective-permute-done((f32[8,8,16,128]{3,2,1,0:T(8,128)S(1)}, f32[8,8,16,128]{3,2,1,0:T(8,128)S(1)}, u32[]{:S(2)}, u32[]{:S(2)}) %collective-permute-start.26) | collective-permute-done | bytes 524320 | tf_op jit(solution)/shard_map/ppermute | solution.py:435
  80.0 1.9 %short_dims.8 = (f32[4,8,16,128]{3,2,1,0:T(8,128)S(1)}, f32[4,8,16,128]{3,2,1,0:T(8,128)S(1)}) custom-call(bf16[64,256]{1,0:T(8,128)(2,1)S(1)} %get-tuple-element.85.kron_hi, bf16[64,256]{1,0:T(8,128)(2,1)S(1)} %get-tuple-element.120.kron_lo, bf16[8,256,256]{2,1,0:T(8,128)(2,1)S(1)} %get-tuple-element.56.right3, f32[16,64,128]{2,1,0:T(8,128)S(1)} %bitcast.33, ...), custom_call_target="tpu_custom_call" | custom-call | flops 1000000 | bytes 10000 | tf_op jit(solution)/shard_map/short_dims/pallas_call | solution.py:453
  82.5 1.5 %collective-permute-start.24 = (f32[4,8,16,128]{3,2,1,0:T(8,128)S(1)}, f32[4,8,16,128]{3,2,1,0:T(8,128)S(1)}, u32[]{:S(2)}, u32[]{:S(2)}) collective-permute-start(f32[4,8,16,128]{3,2,1,0:T(8,128)S(1)} %get-tuple-element.83), channel_id=1, source_target_pairs={{0,1},{1,0},{2,3},{3,2},{4,5},{5,4},{6,7},{7,6},{8,9},{9,8},{10,11... | collective-permute-start | bytes 786440 | tf_op jit(solution)/shard_map/ppermute | solution.py:499
  84.0 1.9 %short_dims.9 = (f32[4,8,16,128]{3,2,1,0:T(8,128)S(1)}, f32[4,8,16,128]{3,2,1,0:T(8,128)S(1)}) custom-call(bf16[64,256]{1,0:T(8,128)(2,1)S(1)} %get-tuple-element.91.kron_hi, bf16[64,256]{1,0:T(8,128)(2,1)S(1)} %get-tuple-element.119.kron_lo, bf16[8,256,256]{2,1,0:T(8,128)(2,1)S(1)} %get-tuple-element.56.right3, f32[16,64,128]{2,1,0:T(8,128)S(1)} %bitcast.34, ...), custom_call_target="tpu_custom_call" | custom-call | flops 1000000 | bytes 10000 | tf_op jit(solution)/shard_map/short_dims/pallas_call | solution.py:453
  86.0 4.5 %collective-permute-done.31.refs_7_ = f32[4,8,16,128]{3,2,1,0:T(8,128)S(1)} collective-permute-done((f32[4,8,16,128]{3,2,1,0:T(8,128)S(1)}, f32[4,8,16,128]{3,2,1,0:T(8,128)S(1)}, u32[]{:S(2)}, u32[]{:S(2)}) %collective-permute-start.31) | collective-permute-done | bytes 262176 | tf_op jit(solution)/shard_map/ppermute | solution.py:519
  91.1 1.8 %third_dim.3 = (f32[4,8,128,128]{3,2,1,0:T(8,128)S(1)}, f32[8,128,128]{2,1,0:T(8,128)S(1)}) custom-call(s32[44]{0:T(128)S(1)} %concatenate.34.meta, f32[8,16]{1,0:T(8,128)S(1)} %copy-done, f32[8,16]{1,0:T(8,128)S(1)} %copy-done.1, bf16[4,256,256]{2,1,0:T(8,128)(2,1)S(1)} %get-tuple-element.52.left2, f32[4,128,128]{2,1,0:T(8,128)S(1)} %get-tuple-element.53.util23, ...), custom_call_target="tpu_custom_call" | custom-call | flops 1000000000 | bytes 5000000 | tf_op jit(solution)/shard_map/third_dim/pallas_call | solution.py:534
  92.9 1.6 %collective-permute-start.34 = (f32[8,128,128]{2,1,0:T(8,128)S(1)}, f32[8,128,128]{2,1,0:T(8,128)S(1)}, u32[]{:S(2)}, u32[]{:S(2)}) collective-permute-start(f32[8,128,128]{2,1,0:T(8,128)S(1)} %get-tuple-element.99.mine), channel_id=1, source_target_pairs={{0,1},{1,0},{2,3},{3,2},{4,5},{5,4},{6,7},{7,6},{8,9},{9,8},{10,11... | collective-permute-start | bytes 1572872 | tf_op jit(solution)/shard_map/ppermute | solution.py:549
  94.4 3.8 %collective-permute-done.32.refs_7_ = f32[4,8,16,128]{3,2,1,0:T(8,128)S(1)} collective-permute-done((f32[4,8,16,128]{3,2,1,0:T(8,128)S(1)}, f32[4,8,16,128]{3,2,1,0:T(8,128)S(1)}, u32[]{:S(2)}, u32[]{:S(2)}) %collective-permute-start.32) | collective-permute-done | bytes 262176 | tf_op jit(solution)/shard_map/ppermute | solution.py:519
  98.2 1.8 %third_dim.2 = (f32[4,8,128,128]{3,2,1,0:T(8,128)S(1)}, f32[8,128,128]{2,1,0:T(8,128)S(1)}) custom-call(s32[44]{0:T(128)S(1)} %concatenate.34.meta, f32[8,16]{1,0:T(8,128)S(1)} %copy-done, f32[8,16]{1,0:T(8,128)S(1)} %copy-done.1, bf16[4,256,256]{2,1,0:T(8,128)(2,1)S(1)} %get-tuple-element.52.left2, f32[4,128,128]{2,1,0:T(8,128)S(1)} %get-tuple-element.53.util23, ...), custom_call_target="tpu_custom_call" | custom-call | flops 1000000000 | bytes 5000000 | tf_op jit(solution)/shard_map/third_dim/pallas_call | solution.py:534
  100.0 1.5 %collective-permute-start.33 = (f32[8,128,128]{2,1,0:T(8,128)S(1)}, f32[8,128,128]{2,1,0:T(8,128)S(1)}, u32[]{:S(2)}, u32[]{:S(2)}) collective-permute-start(f32[8,128,128]{2,1,0:T(8,128)S(1)} %get-tuple-element.96.mine), channel_id=1, source_target_pairs={{0,1},{1,0},{2,3},{3,2},{4,5},{5,4},{6,7},{7,6},{8,9},{9,8},{10,11... | collective-permute-start | bytes 1572872 | tf_op jit(solution)/shard_map/ppermute | solution.py:549
  101.6 6.3 %collective-permute-done.34.other = f32[8,128,128]{2,1,0:T(8,128)S(1)} collective-permute-done((f32[8,128,128]{2,1,0:T(8,128)S(1)}, f32[8,128,128]{2,1,0:T(8,128)S(1)}, u32[]{:S(2)}, u32[]{:S(2)}) %collective-permute-start.34) | collective-permute-done | bytes 524320 | tf_op jit(solution)/shard_map/ppermute | solution.py:549
  107.8 1.4 %choice.2 = (f32[2,8,128,128]{3,2,1,0:T(8,128)}, bf16[4,2,8,128,128]{4,3,2,1,0:T(8,128)(2,1)}) custom-call(f32[4,8,128,128]{3,2,1,0:T(8,128)S(1)} %get-tuple-element.98.scores, f32[8,128,128]{2,1,0:T(8,128)S(1)} %get-tuple-element.99.mine, f32[8,128,128]{2,1,0:T(8,128)S(1)} %collective-permute-done.34.other), custom_call_target="tpu_custom_call" | custom-call | flops 10000000 | bytes 5000000 | tf_op jit(solution)/shard_map/choice/pallas_call | solution.py:553
  109.3 8.0 %collective-permute-done.33.other = f32[8,128,128]{2,1,0:T(8,128)S(1)} collective-permute-done((f32[8,128,128]{2,1,0:T(8,128)S(1)}, f32[8,128,128]{2,1,0:T(8,128)S(1)}, u32[]{:S(2)}, u32[]{:S(2)}) %collective-permute-start.33) | collective-permute-done | bytes 524320 | tf_op jit(solution)/shard_map/ppermute | solution.py:549
  117.3 1.5 %choice.3 = (f32[2,8,128,128]{3,2,1,0:T(8,128)}, bf16[4,2,8,128,128]{4,3,2,1,0:T(8,128)(2,1)}) custom-call(f32[4,8,128,128]{3,2,1,0:T(8,128)S(1)} %get-tuple-element.95.scores, f32[8,128,128]{2,1,0:T(8,128)S(1)} %get-tuple-element.96.mine, f32[8,128,128]{2,1,0:T(8,128)S(1)} %collective-permute-done.33.other, ...), custom_call_target="tpu_custom_call", output_to_operand_aliasing={{0}: (3, {}), {1}: (4, {})} | custom-call | flops 10000000 | bytes 5000000 | tf_op jit(solution)/shard_map/choice/pallas_call | solution.py:553
  (87 shorter events, 19.2 us)
Async XLA Ops:
  2.0 15.3 %collective-permute-start = (f32[2,8,16,128]{3,2,1,0:T(8,128)S(1)}, f32[2,8,16,128]{3,2,1,0:T(8,128)S(1)}, u32[]{:S(2)}, u32[]{:S(2)}) collective-permute-start(f32[2,8,16,128]{3,2,1,0:T(8,128)S(1)} %get-tuple-element.107), channel_id=1, source_target_pairs={{0,8},{4,12},{8,0},{12,4},{16,24},{20,28},{24,16},{28,20},{1,9},{5... | collective-permute-start | bytes 393224 | tf_op jit(solution)/shard_map/ppermute | solution.py:411
  5.1 12.9 %collective-permute-start.1 = (f32[2,8,16,128]{3,2,1,0:T(8,128)S(1)}, f32[2,8,16,128]{3,2,1,0:T(8,128)S(1)}, u32[]{:S(2)}, u32[]{:S(2)}) collective-permute-start(f32[2,8,16,128]{3,2,1,0:T(8,128)S(1)} %get-tuple-element.107), channel_id=1, source_target_pairs={{0,16},{4,20},{8,24},{12,28},{16,0},{20,4},{24,8},{28,12},{1,17},{... | collective-permute-start | bytes 393224 | tf_op jit(solution)/shard_map/ppermute | solution.py:411
  7.7 10.3 %collective-permute-start.2 = (f32[2,8,16,128]{3,2,1,0:T(8,128)S(1)}, f32[2,8,16,128]{3,2,1,0:T(8,128)S(1)}, u32[]{:S(2)}, u32[]{:S(2)}) collective-permute-start(f32[2,8,16,128]{3,2,1,0:T(8,128)S(1)} %get-tuple-element.107), channel_id=1, source_target_pairs={{0,24},{4,28},{8,16},{12,20},{16,8},{20,12},{24,0},{28,4},{1,25},{... | collective-permute-start | bytes 393224 | tf_op jit(solution)/shard_map/ppermute | solution.py:411
  8.9 14.1 %collective-permute-start.5 = (f32[2,8,64,128]{3,2,1,0:T(8,128)S(1)}, f32[2,8,64,128]{3,2,1,0:T(8,128)S(1)}, u32[]{:S(2)}, u32[]{:S(2)}) collective-permute-start(f32[2,8,64,128]{3,2,1,0:T(8,128)S(1)} %get-tuple-element.109), channel_id=1, source_target_pairs={{0,2},{2,0},{1,3},{3,1},{4,6},{6,4},{5,7},{7,5},{8,10},{10,8},{9,1... | collective-permute-start | bytes 1572872 | tf_op jit(solution)/shard_map/ppermute | solution.py:412
  11.7 10.4 %collective-permute-start.9 = (f32[2,8,32,128]{3,2,1,0:T(8,128)S(1)}, f32[2,8,32,128]{3,2,1,0:T(8,128)S(1)}, u32[]{:S(2)}, u32[]{:S(2)}) collective-permute-start(f32[2,8,32,128]{3,2,1,0:T(8,128)S(1)} %constant_dynamic-slice_fusion.2), channel_id=1, source_target_pairs={{0,8},{4,12},{8,0},{12,4},{16,24},{20,28},{24,16},{28,20},{1,9},{5... | collective-permute-start | bytes 786440 | tf_op jit(solution)/shard_map/ppermute | solution.py:413
  18.1 8.8 %collective-permute-start.3 = (f32[6,8,16,128]{3,2,1,0:T(8,128)S(1)}, f32[6,8,16,128]{3,2,1,0:T(8,128)S(1)}, u32[]{:S(2)}, u32[]{:S(2)}) collective-permute-start(f32[6,8,16,128]{3,2,1,0:T(8,128)S(1)} %constant_dynamic-update-slice_fusion), channel_id=1, source_target_pairs={{0,4},{4,0},{8,12},{12,8},{16,20},{20,16},{24,28},{28,24},{1,5},{5... | collective-permute-start | bytes 1179656 | tf_op jit(solution)/shard_map/ppermute | solution.py:443
  18.2 12.3 %collective-permute-start.7 = (f32[6,8,16,128]{3,2,1,0:T(8,128)S(1)}, f32[6,8,16,128]{3,2,1,0:T(8,128)S(1)}, u32[]{:S(2)}, u32[]{:S(2)}) collective-permute-start(f32[6,8,16,128]{3,2,1,0:T(8,128)S(1)} %constant_dynamic-update-slice_fusion), channel_id=1, source_target_pairs={{0,2},{2,0},{1,3},{3,1},{4,6},{6,4},{5,7},{7,5},{8,10},{10,8},{9,1... | collective-permute-start | bytes 1179656 | tf_op jit(solution)/shard_map/ppermute | solution.py:444
  22.1 14.0 %collective-permute-start.10 = (f32[4,8,16,128]{3,2,1,0:T(8,128)S(1)}, f32[4,8,16,128]{3,2,1,0:T(8,128)S(1)}, u32[]{:S(2)}, u32[]{:S(2)}) collective-permute-start(f32[4,8,16,128]{3,2,1,0:T(8,128)S(1)} %pad_maximum_fusion.5), channel_id=1, source_target_pairs={{0,16},{4,20},{8,24},{12,28},{16,0},{20,4},{24,8},{28,12},{1,17},{... | collective-permute-start | bytes 786440 | tf_op jit(solution)/shard_map/ppermute | solution.py:424
  23.0 13.3 %collective-permute-start.11 = (f32[4,8,16,128]{3,2,1,0:T(8,128)S(1)}, f32[4,8,16,128]{3,2,1,0:T(8,128)S(1)}, u32[]{:S(2)}, u32[]{:S(2)}) collective-permute-start(f32[4,8,16,128]{3,2,1,0:T(8,128)S(1)} %pad_maximum_fusion.6), channel_id=1, source_target_pairs={{0,8},{4,12},{8,0},{12,4},{16,24},{20,28},{24,16},{28,20},{1,9},{5... | collective-permute-start | bytes 786440 | tf_op jit(solution)/shard_map/ppermute | solution.py:445
  26.9 10.0 %collective-permute-start.4 = (f32[2,8,64,128]{3,2,1,0:T(8,128)S(1)}, f32[2,8,64,128]{3,2,1,0:T(8,128)S(1)}, u32[]{:S(2)}, u32[]{:S(2)}) collective-permute-start(f32[2,8,64,128]{3,2,1,0:T(8,128)S(1)} %get-tuple-element.63), channel_id=1, source_target_pairs={{0,4},{4,0},{8,12},{12,8},{16,20},{20,16},{24,28},{28,24},{1,5},{5... | collective-permute-start | bytes 1572872 | tf_op jit(solution)/shard_map/ppermute | solution.py:448
  27.0 10.4 %collective-permute-start.6 = (f32[2,8,64,128]{3,2,1,0:T(8,128)S(1)}, f32[2,8,64,128]{3,2,1,0:T(8,128)S(1)}, u32[]{:S(2)}, u32[]{:S(2)}) collective-permute-start(f32[2,8,64,128]{3,2,1,0:T(8,128)S(1)} %collective-permute-done.5), channel_id=1, source_target_pairs={{0,4},{4,0},{8,12},{12,8},{16,20},{20,16},{24,28},{28,24},{1,5},{5... | collective-permute-start | bytes 1572872 | tf_op jit(solution)/shard_map/ppermute | solution.py:449
  30.5 6.4 %collective-permute-start.8 = (f32[6,8,16,128]{3,2,1,0:T(8,128)S(1)}, f32[6,8,16,128]{3,2,1,0:T(8,128)S(1)}, u32[]{:S(2)}, u32[]{:S(2)}) collective-permute-start(f32[6,8,16,128]{3,2,1,0:T(8,128)S(1)} %collective-permute-done.7), channel_id=1, source_target_pairs={{0,4},{4,0},{8,12},{12,8},{16,20},{20,16},{24,28},{28,24},{1,5},{5... | collective-permute-start | bytes 1179656 | tf_op jit(solution)/shard_map/ppermute | solution.py:485
  36.1 14.1 %collective-permute-start.17 = (f32[4,8,16,128]{3,2,1,0:T(8,128)S(1)}, f32[4,8,16,128]{3,2,1,0:T(8,128)S(1)}, u32[]{:S(2)}, u32[]{:S(2)}) collective-permute-start(f32[4,8,16,128]{3,2,1,0:T(8,128)S(1)} %pad_maximum_fusion.7), channel_id=1, source_target_pairs={{0,16},{4,20},{8,24},{12,28},{16,0},{20,4},{24,8},{28,12},{1,17},{... | collective-permute-start | bytes 786440 | tf_op jit(solution)/shard_map/ppermute | solution.py:424
  36.3 14.0 %collective-permute-start.13 = (f32[6,8,16,128]{3,2,1,0:T(8,128)S(1)}, f32[6,8,16,128]{3,2,1,0:T(8,128)S(1)}, u32[]{:S(2)}, u32[]{:S(2)}) collective-permute-start(f32[6,8,16,128]{3,2,1,0:T(8,128)S(1)} %pad_maximum_fusion.3), channel_id=1, source_target_pairs={{0,2},{2,0},{1,3},{3,1},{4,6},{6,4},{5,7},{7,5},{8,10},{10,8},{9,1... | collective-permute-start | bytes 1179656 | tf_op jit(solution)/shard_map/ppermute | solution.py:479
  36.8 14.2 %collective-permute-start.14 = (f32[2,8,16,128]{3,2,1,0:T(8,128)S(1)}, f32[2,8,16,128]{3,2,1,0:T(8,128)S(1)}, u32[]{:S(2)}, u32[]{:S(2)}) collective-permute-start(f32[2,8,16,128]{3,2,1,0:T(8,128)S(1)} %get-tuple-element.118), channel_id=1, source_target_pairs={{0,4},{4,0},{8,12},{12,8},{16,20},{20,16},{24,28},{28,24},{1,5},{5... | collective-permute-start | bytes 393224 | tf_op jit(solution)/shard_map/ppermute | solution.py:470
  36.9 14.2 %collective-permute-start.15 = (f32[2,8,16,128]{3,2,1,0:T(8,128)S(1)}, f32[2,8,16,128]{3,2,1,0:T(8,128)S(1)}, u32[]{:S(2)}, u32[]{:S(2)}) collective-permute-start(f32[2,8,16,128]{3,2,1,0:T(8,128)S(1)} %get-tuple-element.117), channel_id=1, source_target_pairs={{0,4},{4,0},{8,12},{12,8},{16,20},{20,16},{24,28},{28,24},{1,5},{5... | collective-permute-start | bytes 393224 | tf_op jit(solution)/shard_map/ppermute | solution.py:470
  39.7 15.9 %collective-permute-start.21 = (f32[4,16,16,128]{3,2,1,0:T(8,128)S(1)}, f32[4,16,16,128]{3,2,1,0:T(8,128)S(1)}, u32[]{:S(2)}, u32[]{:S(2)}) collective-permute-start(f32[4,16,16,128]{3,2,1,0:T(8,128)S(1)} %get-tuple-element.77), channel_id=1, source_target_pairs={{0,1},{1,0},{2,3},{3,2},{4,5},{5,4},{6,7},{7,6},{8,9},{9,8},{10,11... | collective-permute-start | bytes 1572872 | tf_op jit(solution)/shard_map/ppermute | solution.py:499
  50.3 12.4 %collective-permute-start.25 = (f32[8,8,16,128]{3,2,1,0:T(8,128)S(1)}, f32[8,8,16,128]{3,2,1,0:T(8,128)S(1)}, u32[]{:S(2)}, u32[]{:S(2)}) collective-permute-start(f32[8,8,16,128]{3,2,1,0:T(8,128)S(1)} %pad_maximum_fusion.2), channel_id=1, source_target_pairs={{8,16},{12,20},{16,8},{20,12},{9,17},{13,21},{17,9},{21,13},{10,18... | collective-permute-start | bytes 1572872 | tf_op jit(solution)/shard_map/ppermute | solution.py:434
  51.0 1.8 %collective-permute-start.12 = (f32[6,8,16,128]{3,2,1,0:T(8,128)S(1)}, f32[6,8,16,128]{3,2,1,0:T(8,128)S(1)}, u32[]{:S(2)}, u32[]{:S(2)}) collective-permute-start(f32[6,8,16,128]{3,2,1,0:T(8,128)S(1)} %pad_maximum_fusion.3), channel_id=1, source_target_pairs={{0,4},{4,0},{8,12},{12,8},{16,20},{20,16},{24,28},{28,24},{1,5},{5... | collective-permute-start | bytes 1179656 | tf_op jit(solution)/shard_map/ppermute | solution.py:478
  51.1 2.3 %collective-permute-start.16 = (f32[6,8,16,128]{3,2,1,0:T(8,128)S(1)}, f32[6,8,16,128]{3,2,1,0:T(8,128)S(1)}, u32[]{:S(2)}, u32[]{:S(2)}) collective-permute-start(f32[6,8,16,128]{3,2,1,0:T(8,128)S(1)} %collective-permute-done.13), channel_id=1, source_target_pairs={{0,4},{4,0},{8,12},{12,8},{16,20},{20,16},{24,28},{28,24},{1,5},{5... | collective-permute-start | bytes 1179656 | tf_op jit(solution)/shard_map/ppermute | solution.py:485
  51.6 11.1 %collective-permute-start.19 = (f32[6,8,16,128]{3,2,1,0:T(8,128)S(1)}, f32[6,8,16,128]{3,2,1,0:T(8,128)S(1)}, u32[]{:S(2)}, u32[]{:S(2)}) collective-permute-start(f32[6,8,16,128]{3,2,1,0:T(8,128)S(1)} %pad_maximum_fusion.4), channel_id=1, source_target_pairs={{0,2},{2,0},{1,3},{3,1},{4,6},{6,4},{5,7},{7,5},{8,10},{10,8},{9,1... | collective-permute-start | bytes 1179656 | tf_op jit(solution)/shard_map/ppermute | solution.py:479
  55.6 14.0 %collective-permute-start.22 = (f32[4,16,16,128]{3,2,1,0:T(8,128)S(1)}, f32[4,16,16,128]{3,2,1,0:T(8,128)S(1)}, u32[]{:S(2)}, u32[]{:S(2)}) collective-permute-start(f32[4,16,16,128]{3,2,1,0:T(8,128)S(1)} %get-tuple-element.79), channel_id=1, source_target_pairs={{0,1},{1,0},{2,3},{3,2},{4,5},{5,4},{6,7},{7,6},{8,9},{9,8},{10,11... | collective-permute-start | bytes 1572872 | tf_op jit(solution)/shard_map/ppermute | solution.py:499
  62.7 15.0 %collective-permute-start.26 = (f32[8,8,16,128]{3,2,1,0:T(8,128)S(1)}, f32[8,8,16,128]{3,2,1,0:T(8,128)S(1)}, u32[]{:S(2)}, u32[]{:S(2)}) collective-permute-start(f32[8,8,16,128]{3,2,1,0:T(8,128)S(1)} %collective-permute-done.25), channel_id=1, source_target_pairs={{8,0},{12,4},{16,24},{20,28},{9,1},{13,5},{17,25},{21,29},{10,2},{... | collective-permute-start | bytes 1572872 | tf_op jit(solution)/shard_map/ppermute | solution.py:435
  64.2 1.8 %collective-permute-start.18 = (f32[6,8,16,128]{3,2,1,0:T(8,128)S(1)}, f32[6,8,16,128]{3,2,1,0:T(8,128)S(1)}, u32[]{:S(2)}, u32[]{:S(2)}) collective-permute-start(f32[6,8,16,128]{3,2,1,0:T(8,128)S(1)} %pad_maximum_fusion.4), channel_id=1, source_target_pairs={{0,4},{4,0},{8,12},{12,8},{16,20},{20,16},{24,28},{28,24},{1,5},{5... | collective-permute-start | bytes 1179656 | tf_op jit(solution)/shard_map/ppermute | solution.py:478
  64.2 2.3 %collective-permute-start.20 = (f32[6,8,16,128]{3,2,1,0:T(8,128)S(1)}, f32[6,8,16,128]{3,2,1,0:T(8,128)S(1)}, u32[]{:S(2)}, u32[]{:S(2)}) collective-permute-start(f32[6,8,16,128]{3,2,1,0:T(8,128)S(1)} %collective-permute-done.19), channel_id=1, source_target_pairs={{0,4},{4,0},{8,12},{12,8},{16,20},{20,16},{24,28},{28,24},{1,5},{5... | collective-permute-start | bytes 1179656 | tf_op jit(solution)/shard_map/ppermute | solution.py:485
  69.7 9.3 %collective-permute-start.23 = (f32[4,8,16,128]{3,2,1,0:T(8,128)S(1)}, f32[4,8,16,128]{3,2,1,0:T(8,128)S(1)}, u32[]{:S(2)}, u32[]{:S(2)}) collective-permute-start(f32[4,8,16,128]{3,2,1,0:T(8,128)S(1)} %get-tuple-element.82), channel_id=1, source_target_pairs={{0,1},{1,0},{2,3},{3,2},{4,5},{5,4},{6,7},{7,6},{8,9},{9,8},{10,11... | collective-permute-start | bytes 786440 | tf_op jit(solution)/shard_map/ppermute | solution.py:499
  77.8 1.5 %collective-permute-start.28 = (f32[2,8,16,128]{3,2,1,0:T(8,128)S(1)}, f32[2,8,16,128]{3,2,1,0:T(8,128)S(1)}, u32[]{:S(2)}, u32[]{:S(2)}) collective-permute-start(f32[2,8,16,128]{3,2,1,0:T(8,128)S(1)} %get-tuple-element.113), channel_id=1, source_target_pairs={{0,4},{4,0},{8,12},{12,8},{16,20},{20,16},{24,28},{28,24},{1,5},{5... | collective-permute-start | bytes 393224 | tf_op jit(solution)/shard_map/ppermute | solution.py:502
  81.9 8.6 %collective-permute-start.31 = (f32[4,8,16,128]{3,2,1,0:T(8,128)S(1)}, f32[4,8,16,128]{3,2,1,0:T(8,128)S(1)}, u32[]{:S(2)}, u32[]{:S(2)}) collective-permute-start(f32[4,8,16,128]{3,2,1,0:T(8,128)S(1)} %get-tuple-element.90), channel_id=1, source_target_pairs={{0,2},{2,0},{1,3},{3,1},{4,6},{6,4},{5,7},{7,5},{8,10},{10,8},{9,1... | collective-permute-start | bytes 786440 | tf_op jit(solution)/shard_map/ppermute | solution.py:519
  82.5 11.9 %collective-permute-start.24 = (f32[4,8,16,128]{3,2,1,0:T(8,128)S(1)}, f32[4,8,16,128]{3,2,1,0:T(8,128)S(1)}, u32[]{:S(2)}, u32[]{:S(2)}) collective-permute-start(f32[4,8,16,128]{3,2,1,0:T(8,128)S(1)} %get-tuple-element.83), channel_id=1, source_target_pairs={{0,1},{1,0},{2,3},{3,2},{4,5},{5,4},{6,7},{7,6},{8,9},{9,8},{10,11... | collective-permute-start | bytes 786440 | tf_op jit(solution)/shard_map/ppermute | solution.py:499
  90.5 7.7 %collective-permute-start.32 = (f32[4,8,16,128]{3,2,1,0:T(8,128)S(1)}, f32[4,8,16,128]{3,2,1,0:T(8,128)S(1)}, u32[]{:S(2)}, u32[]{:S(2)}) collective-permute-start(f32[4,8,16,128]{3,2,1,0:T(8,128)S(1)} %get-tuple-element.94), channel_id=1, source_target_pairs={{0,2},{2,0},{1,3},{3,1},{4,6},{6,4},{5,7},{7,5},{8,10},{10,8},{9,1... | collective-permute-start | bytes 786440 | tf_op jit(solution)/shard_map/ppermute | solution.py:519
  92.9 14.9 %collective-permute-start.34 = (f32[8,128,128]{2,1,0:T(8,128)S(1)}, f32[8,128,128]{2,1,0:T(8,128)S(1)}, u32[]{:S(2)}, u32[]{:S(2)}) collective-permute-start(f32[8,128,128]{2,1,0:T(8,128)S(1)} %get-tuple-element.99.mine), channel_id=1, source_target_pairs={{0,1},{1,0},{2,3},{3,2},{4,5},{5,4},{6,7},{7,6},{8,9},{9,8},{10,11... | collective-permute-start | bytes 1572872 | tf_op jit(solution)/shard_map/ppermute | solution.py:549
  100.0 17.2 %collective-permute-start.33 = (f32[8,128,128]{2,1,0:T(8,128)S(1)}, f32[8,128,128]{2,1,0:T(8,128)S(1)}, u32[]{:S(2)}, u32[]{:S(2)}) collective-permute-start(f32[8,128,128]{2,1,0:T(8,128)S(1)} %get-tuple-element.96.mine), channel_id=1, source_target_pairs={{0,1},{1,0},{2,3},{3,2},{4,5},{5,4},{6,7},{7,6},{8,9},{9,8},{10,11... | collective-permute-start | bytes 1572872 | tf_op jit(solution)/shard_map/ppermute | solution.py:549
  (10 other events, 70.2 us)
where the time goes:
time: 119 us
  waiting for transfers between devices  60.6 us (51%)
  starting transfers between devices  29.8 us (25%)
  Pallas kernels  23.2 us (19%)
  local copies, waits for them, and re-layouts  3.74 us (3%)
    ppermute x2, waiting for transfers between devices, doubled(): more = lax.ppermute(grown, 'wide', across(bit))  14.7 us
    ppermute x2, waiting for transfers between devices, gather_body(): by_row.append((scores, local, lax.ppermute(local, 'act', act_flip)))  14.2 us
    pallas_call x5, Pallas kernels, contract(): pl.pallas_call(functools.partial(short_dims_kernel, views, routes), out_s...  10.6 us
    ppermute x2, waiting for transfers between devices, gather_body(): lax.ppermute(after(give, *side_got[-1:]), 'narrow', narrow_flip)  8.28 us
    ppermute x1, waiting for transfers between devices, by_line(): passed = lax.ppermute(after(came, moved[-1]), 'wide', outward)  6.51 us
    ppermute x4, starting transfers between devices, gather_body(): sent[-1].append(lax.ppermute(after(one, *before), 'act', act_flip))  5.99 us
    ppermute x3, starting transfers between devices, gather_body(): lax.ppermute(chunks[0], 'wide', across(far))  5.68 us
    ppermute x2, waiting for transfers between devices, gather_body(): moved.append(lax.ppermute(after(far, moved[-1]), 'narrow', narrow_flip))  5.51 us
  transfers between devices with their start and end apart: 35, of which 21 were waited for; matrix products, arithmetic and copies ran while one was open for 2% of the time, Pallas kernels for 17%

commit v1 on v0

--- a/solution.py
+++ b/solution.py
@@ -259,14 +259,14 @@
                 first += count
 
 
-def third_dim_kernel(n_pieces, rows0, row, meta, costs0, costs1, left2, util23, *refs):
+def third_dim_kernel(n_pieces, rows0, row, pieces1, piece1, meta, costs0, costs1, left2, util23, *refs):
     pieces, scores, local = refs[:n_pieces], refs[n_pieces], refs[n_pieces + 1]
     per_group, rows1 = scores.shape[:2]
     length = util23.shape[1]
     depth = util23.shape[2]
     which = [meta[PLACE + meta[0] * per_group + slot] for slot in range(per_group)]
     first = (meta[2] * 2 + meta[3]) * rows0 + row
-    start1 = meta[1] * rows1
+    start1 = (meta[1] * pieces1 + piece1) * rows1
     for second in range(0, rows1, 2):
         for slot in range(per_group):
             cols = [
@@ -522,21 +522,23 @@
     parts = [(keep, None) for keep in kept] + [(ones[0], None) for ones in sent[:-1]]
     parts += [(sent[-1][0], sent[-1]), (side_keep[0], side_keep), (side_got[0], side_got)]
     by_row = []
-    for row in range(rows0):
+    units = [(row, piece) for row in range(rows0) for piece in range(2)]
+    unit1 = rows1 // 2
+    for row, piece in units:
         arrays = [cut[row] if cut else one for one, cut in parts]
         specs = [
             pl.BlockSpec(
-                (per_group, rows1) + one.shape[2:],
-                lambda i, block=0 if cut else row: (0, block, 0, 0),
+                (per_group, unit1) + one.shape[2:],
+                lambda i, block=piece if cut else 2 * row + piece: (0, block, 0, 0),
             )
             for one, (_, cut) in zip(arrays, parts)
         ]
         scores, local = pl.pallas_call(
-            functools.partial(third_dim_kernel, len(parts), rows0, row),
+            functools.partial(third_dim_kernel, len(parts), rows0, row, 2, piece),
             grid=(1,),
             out_shape=(
-                jax.ShapeDtypeStruct((per_group, rows1, len2, len3), F32),
-                jax.ShapeDtypeStruct((rows1, len2, len3), F32),
+                jax.ShapeDtypeStruct((per_group, unit1, len2, len3), F32),
+                jax.ShapeDtypeStruct((unit1, len2, len3), F32),
             ),
             in_specs=[smem] * 3 + [whole_block()] * 2 + specs,
             out_specs=(whole_block(),) * 2,
@@ -549,7 +551,7 @@
         by_row.append((scores, local, lax.ppermute(local, "act", act_flip)))
 
     results = ()
-    for row, operands in enumerate(by_row):
+    for (row, piece), operands in zip(units, by_row):
         results = pl.pallas_call(
             choice_kernel,
             grid=(1,),
@@ -559,9 +561,9 @@
             ),
             in_specs=[whole_block()] * 3 + [pl.BlockSpec(memory_space=pl.ANY)] * len(results),
             out_specs=(
-                pl.BlockSpec((1, rows1, len2, len3), lambda i, row=row: (row, 0, 0, 0)),
+                pl.BlockSpec((1, unit1, len2, len3), lambda i, at=(row, piece): at + (0, 0)),
                 pl.BlockSpec(
-                    (per_group, 1, rows1, len2, len3), lambda i, row=row: (0, row, 0, 0, 0)
+                    (per_group, 1, unit1, len2, len3), lambda i, at=(row, piece): (0,) + at + (0, 0)
                 ),
             ),
             input_output_aliases={3: 0, 4: 1} if results else {},

time: 119 us -> 118 us (level)
  waiting for transfers between devices: 60.6 us -> 55.8 us
  Pallas kernels: 23.2 us -> 25.9 us
  starting transfers between devices: 29.8 us -> 31 us
    ppermute x2 -> x4, waiting for transfers between devices: 14.2 us -> 10.7 us  [gather_body(): by_row.append((scores, local, lax.ppermute(local, 'act', act_flip)))]
    pallas_call x2 -> x4, Pallas kernels: 3.59 us -> 5.01 us  [gather_body(): pl.pallas_call(functools.partial(third_dim_kernel, len(parts), rows0, row...]
    ppermute x2, waiting for transfers between devices: 8.28 us -> 6.93 us  [gather_body(): lax.ppermute(after(give, *side_got[-1:]), 'narrow', narrow_flip)]
    pallas_call x2 -> x4, Pallas kernels: 2.9 us -> 4.14 us  [gather_body(): pl.pallas_call(choice_kernel, grid=(1,), out_shape=(jax.ShapeDtypeStruct(...]
    ppermute x2 -> x4, starting transfers between devices: 3.1 us -> 4.32 us  [gather_body(): by_row.append((scores, local, lax.ppermute(local, 'act', act_flip)))]
  transfers between devices with their start and end apart: 35 -> 37, of which waited for: 21 -> 22; matrix products, arithmetic and copies ran while one was open for 2% -> 2% of each run, Pallas kernels for 17% -> 19%
where the time goes in v1:
time: 118 us
  waiting for transfers between devices  55.8 us (47%)
  starting transfers between devices  31 us (26%)
  Pallas kernels  25.9 us (22%)
  local copies, waits for them, and re-layouts  3.74 us (3%)
    ppermute x2, waiting for transfers between devices, doubled(): more = lax.ppermute(grown, 'wide', across(bit))  14.7 us
    ppermute x4, waiting for transfers between devices, gather_body(): by_row.append((scores, local, lax.ppermute(local, 'act', act_flip)))  10.7 us
    pallas_call x5, Pallas kernels, contract(): pl.pallas_call(functools.partial(short_dims_kernel, views, routes), out_s...  10.7 us
    ppermute x2, waiting for transfers between devices, gather_body(): lax.ppermute(after(give, *side_got[-1:]), 'narrow', narrow_flip)  6.93 us
    ppermute x1, waiting for transfers between devices, by_line(): passed = lax.ppermute(after(came, moved[-1]), 'wide', outward)  6.51 us
    ppermute x4, starting transfers between devices, gather_body(): sent[-1].append(lax.ppermute(after(one, *before), 'act', act_flip))  5.99 us
    ppermute x3, starting transfers between devices, gather_body(): lax.ppermute(chunks[0], 'wide', across(far))  5.68 us
    ppermute x2, waiting for transfers between devices, gather_body(): moved.append(lax.ppermute(after(far, moved[-1]), 'narrow', narrow_flip))  5.51 us
  transfers between devices with their start and end apart: 37, of which 22 were waited for; matrix products, arithmetic and copies ran while one was open for 2% of the time, Pallas kernels for 19%

profile of v1, /device:TPU:0, one launch (start us, length us, event | category | flops | bytes accessed | tf_op | source)
XLA Modules:
  0.0 117.8 jit_solution(1531653779441066401)
XLA Ops:
  0.7 1.4 %constant_dynamic-slice_fusion = (f32[2,8,16,128]{3,2,1,0:T(8,128)S(1)}, f32[2,8,16,128]{3,2,1,0:T(8,128)S(1)}, f32[2,8,16,128]{3,2,1,0:T(8,128)S(1)}, f32[2,8,16,128]{3,2,1,0:T(8,128)S(1)}, f32[2,8,16,128]{3,2,1,0:T(8,128)S(1)}) fusion(f32[2,8,128,128]{3,2,1,0:T(8,128)} %param.8, s32[]{:T(128)S(6)} %select_n.47, s32[]{:T(128)S(6)} %select_n.46, ...), kind=kLoop, calls=%fused_computation.13 | loop fusion | bytes 1310740 | tf_op jit(solution)/shard_map/dynamic_slice | solution.py:345
  2.0 3.1 %collective-permute-start = (f32[2,8,16,128]{3,2,1,0:T(8,128)S(1)}, f32[2,8,16,128]{3,2,1,0:T(8,128)S(1)}, u32[]{:S(2)}, u32[]{:S(2)}) collective-permute-start(f32[2,8,16,128]{3,2,1,0:T(8,128)S(1)} %get-tuple-element.123), channel_id=1, source_target_pairs={{0,8},{4,12},{8,0},{12,4},{16,24},{20,28},{24,16},{28,20},{1,9},{5... | collective-permute-start | bytes 393224 | tf_op jit(solution)/shard_map/ppermute | solution.py:411
  5.1 2.6 %collective-permute-start.1 = (f32[2,8,16,128]{3,2,1,0:T(8,128)S(1)}, f32[2,8,16,128]{3,2,1,0:T(8,128)S(1)}, u32[]{:S(2)}, u32[]{:S(2)}) collective-permute-start(f32[2,8,16,128]{3,2,1,0:T(8,128)S(1)} %get-tuple-element.123), channel_id=1, source_target_pairs={{0,16},{4,20},{8,24},{12,28},{16,0},{20,4},{24,8},{28,12},{1,17},{... | collective-permute-start | bytes 393224 | tf_op jit(solution)/shard_map/ppermute | solution.py:411
  8.9 1.8 %collective-permute-start.5 = (f32[2,8,64,128]{3,2,1,0:T(8,128)S(1)}, f32[2,8,64,128]{3,2,1,0:T(8,128)S(1)}, u32[]{:S(2)}, u32[]{:S(2)}) collective-permute-start(f32[2,8,64,128]{3,2,1,0:T(8,128)S(1)} %get-tuple-element.125), channel_id=1, source_target_pairs={{0,2},{2,0},{1,3},{3,1},{4,6},{6,4},{5,7},{7,5},{8,10},{10,8},{9,1... | collective-permute-start | bytes 1572872 | tf_op jit(solution)/shard_map/ppermute | solution.py:412
  12.6 4.7 %prepare.1 = (bf16[128,256]{1,0:T(8,128)(2,1)S(1)}, bf16[128,256]{1,0:T(8,128)(2,1)S(1)}, bf16[128,256]{1,0:T(8,128)(2,1)S(1)}, bf16[128,256]{1,0:T(8,128)(2,1)S(1)}, bf16[8,256,256]{2,1,0:T(8,128)(2,1)S(1)}) custom-call(s32[44]{0:T(128)S(1)} %concatenate.34.meta, f32[8,4,256]{2,1,0:T(4,128)S(1)} %pad.4.weights), custom_call_target="tpu_custom_call" | custom-call | flops 1000000000 | bytes 4000000 | tf_op jit(solution)/shard_map/prepare/pallas_call | solution.py:362
  18.2 1.6 %collective-permute-start.7 = (f32[6,8,16,128]{3,2,1,0:T(8,128)S(1)}, f32[6,8,16,128]{3,2,1,0:T(8,128)S(1)}, u32[]{:S(2)}, u32[]{:S(2)}) collective-permute-start(f32[6,8,16,128]{3,2,1,0:T(8,128)S(1)} %constant_dynamic-update-slice_fusion), channel_id=1, source_target_pairs={{0,2},{2,0},{1,3},{3,1},{4,6},{6,4},{5,7},{7,5},{8,10},{10,8},{9,1... | collective-permute-start | bytes 1179656 | tf_op jit(solution)/shard_map/ppermute | solution.py:444
  19.8 2.3 %collective-permute-done.9 = f32[2,8,32,128]{3,2,1,0:T(8,128)S(1)} collective-permute-done((f32[2,8,32,128]{3,2,1,0:T(8,128)S(1)}, f32[2,8,32,128]{3,2,1,0:T(8,128)S(1)}, u32[]{:S(2)}, u32[]{:S(2)}) %collective-permute-start.9) | collective-permute-done | bytes 262176 | tf_op jit(solution)/shard_map/ppermute | solution.py:413
  23.0 2.5 %collective-permute-start.11 = (f32[4,8,16,128]{3,2,1,0:T(8,128)S(1)}, f32[4,8,16,128]{3,2,1,0:T(8,128)S(1)}, u32[]{:S(2)}, u32[]{:S(2)}) collective-permute-start(f32[4,8,16,128]{3,2,1,0:T(8,128)S(1)} %pad_maximum_fusion.6), channel_id=1, source_target_pairs={{0,8},{4,12},{8,0},{12,4},{16,24},{20,28},{24,16},{28,20},{1,9},{5... | collective-permute-start | bytes 786440 | tf_op jit(solution)/shard_map/ppermute | solution.py:445
  25.5 1.3 %prepare_third.1 = (bf16[4,256,256]{2,1,0:T(8,128)(2,1)S(1)}, f32[4,128,128]{2,1,0:T(8,128)S(1)}) custom-call(s32[44]{0:T(128)S(1)} %concatenate.34.meta, f32[8,4,256]{2,1,0:T(4,128)S(1)} %pad.4.weights, f32[8,128]{1,0:T(8,128)S(1)} %copy-done.2, f32[8,128]{1,0:T(8,128)S(1)} %copy-done.3), custom_call_target="tpu_custom_call" | custom-call | flops 1000000000 | bytes 4000000 | tf_op jit(solution)/shard_map/prepare_third/pallas_call | solution.py:382
  27.5 3.0 %collective-permute-done.7 = f32[6,8,16,128]{3,2,1,0:T(8,128)S(1)} collective-permute-done((f32[6,8,16,128]{3,2,1,0:T(8,128)S(1)}, f32[6,8,16,128]{3,2,1,0:T(8,128)S(1)}, u32[]{:S(2)}, u32[]{:S(2)}) %collective-permute-start.7) | collective-permute-done | bytes 393248 | tf_op jit(solution)/shard_map/ppermute | solution.py:444
  30.5 5.6 %collective-permute-done.10 = f32[4,8,16,128]{3,2,1,0:T(8,128)S(1)} collective-permute-done((f32[4,8,16,128]{3,2,1,0:T(8,128)S(1)}, f32[4,8,16,128]{3,2,1,0:T(8,128)S(1)}, u32[]{:S(2)}, u32[]{:S(2)}) %collective-permute-start.10) | collective-permute-done | bytes 262176 | tf_op jit(solution)/shard_map/ppermute | solution.py:424
  37.4 2.3 %short_dims.5 = (f32[4,16,16,128]{3,2,1,0:T(8,128)S(1)}, f32[4,16,16,128]{3,2,1,0:T(8,128)S(1)}) custom-call(bf16[128,256]{1,0:T(8,128)(2,1)S(1)} %get-tuple-element.62.kron_hi, bf16[128,256]{1,0:T(8,128)(2,1)S(1)} %get-tuple-element.63.kron_lo, bf16[8,256,256]{2,1,0:T(8,128)(2,1)S(1)} %get-tuple-element.64.right3, f32[16,64,128]{2,1,0:T(8,128)S(1)} %bitcast.30, ...), custom_call_target="tpu_custom_call" | custom-call | flops 1000000 | bytes 10000 | tf_op jit(solution)/shard_map/short_dims/pallas_call | solution.py:453
  39.7 1.5 %collective-permute-start.21 = (f32[4,16,16,128]{3,2,1,0:T(8,128)S(1)}, f32[4,16,16,128]{3,2,1,0:T(8,128)S(1)}, u32[]{:S(2)}, u32[]{:S(2)}) collective-permute-start(f32[4,16,16,128]{3,2,1,0:T(8,128)S(1)} %get-tuple-element.85), channel_id=1, source_target_pairs={{0,1},{1,0},{2,3},{3,2},{4,5},{5,4},{6,7},{7,6},{8,9},{9,8},{10,11... | collective-permute-start | bytes 1572872 | tf_op jit(solution)/shard_map/ppermute | solution.py:499
  41.2 9.1 %collective-permute-done.17 = f32[4,8,16,128]{3,2,1,0:T(8,128)S(1)} collective-permute-done((f32[4,8,16,128]{3,2,1,0:T(8,128)S(1)}, f32[4,8,16,128]{3,2,1,0:T(8,128)S(1)}, u32[]{:S(2)}, u32[]{:S(2)}) %collective-permute-start.17) | collective-permute-done | bytes 262176 | tf_op jit(solution)/shard_map/ppermute | solution.py:424
  53.3 2.3 %short_dims.6 = (f32[4,16,16,128]{3,2,1,0:T(8,128)S(1)}, f32[4,16,16,128]{3,2,1,0:T(8,128)S(1)}) custom-call(bf16[128,256]{1,0:T(8,128)(2,1)S(1)} %get-tuple-element.62.kron_hi, bf16[128,256]{1,0:T(8,128)(2,1)S(1)} %get-tuple-element.63.kron_lo, bf16[8,256,256]{2,1,0:T(8,128)(2,1)S(1)} %get-tuple-element.64.right3, f32[16,64,128]{2,1,0:T(8,128)S(1)} %bitcast.31, ...), custom_call_target="tpu_custom_call" | custom-call | flops 1000000 | bytes 10000 | tf_op jit(solution)/shard_map/short_dims/pallas_call | solution.py:453
  55.6 1.6 %collective-permute-start.22 = (f32[4,16,16,128]{3,2,1,0:T(8,128)S(1)}, f32[4,16,16,128]{3,2,1,0:T(8,128)S(1)}, u32[]{:S(2)}, u32[]{:S(2)}) collective-permute-start(f32[4,16,16,128]{3,2,1,0:T(8,128)S(1)} %get-tuple-element.87), channel_id=1, source_target_pairs={{0,1},{1,0},{2,3},{3,2},{4,5},{5,4},{6,7},{7,6},{8,9},{9,8},{10,11... | collective-permute-start | bytes 1572872 | tf_op jit(solution)/shard_map/ppermute | solution.py:499
  57.2 5.5 %collective-permute-done.19 = f32[6,8,16,128]{3,2,1,0:T(8,128)S(1)} collective-permute-done((f32[6,8,16,128]{3,2,1,0:T(8,128)S(1)}, f32[6,8,16,128]{3,2,1,0:T(8,128)S(1)}, u32[]{:S(2)}, u32[]{:S(2)}) %collective-permute-start.19) | collective-permute-done | bytes 393248 | tf_op jit(solution)/shard_map/ppermute | solution.py:479
  62.7 1.5 %collective-permute-start.26 = (f32[8,8,16,128]{3,2,1,0:T(8,128)S(1)}, f32[8,8,16,128]{3,2,1,0:T(8,128)S(1)}, u32[]{:S(2)}, u32[]{:S(2)}) collective-permute-start(f32[8,8,16,128]{3,2,1,0:T(8,128)S(1)} %collective-permute-done.25), channel_id=1, source_target_pairs={{8,0},{12,4},{16,24},{20,28},{9,1},{13,5},{17,25},{21,29},{10,2},{... | collective-permute-start | bytes 1572872 | tf_op jit(solution)/shard_map/ppermute | solution.py:435
  66.5 2.3 %short_dims.7 = (f32[4,16,16,128]{3,2,1,0:T(8,128)S(1)}, f32[4,8,16,128]{3,2,1,0:T(8,128)S(1)}, f32[4,8,16,128]{3,2,1,0:T(8,128)S(1)}) custom-call(bf16[128,256]{1,0:T(8,128)(2,1)S(1)} %get-tuple-element.62.kron_hi, bf16[128,256]{1,0:T(8,128)(2,1)S(1)} %get-tuple-element.63.kron_lo, bf16[8,256,256]{2,1,0:T(8,128)(2,1)S(1)} %get-tuple-element.64.right3, ...), custom_call_target="tpu_custom_call" | custom-call | flops 1000000 | bytes 10000 | tf_op jit(solution)/shard_map/short_dims/pallas_call | solution.py:453
  69.7 1.5 %collective-permute-start.23 = (f32[4,8,16,128]{3,2,1,0:T(8,128)S(1)}, f32[4,8,16,128]{3,2,1,0:T(8,128)S(1)}, u32[]{:S(2)}, u32[]{:S(2)}) collective-permute-start(f32[4,8,16,128]{3,2,1,0:T(8,128)S(1)} %get-tuple-element.90), channel_id=1, source_target_pairs={{0,1},{1,0},{2,3},{3,2},{4,5},{5,4},{6,7},{7,6},{8,9},{9,8},{10,11... | collective-permute-start | bytes 786440 | tf_op jit(solution)/shard_map/ppermute | solution.py:499
  71.1 6.5 %collective-permute-done.26 = f32[8,8,16,128]{3,2,1,0:T(8,128)S(1)} collective-permute-done((f32[8,8,16,128]{3,2,1,0:T(8,128)S(1)}, f32[8,8,16,128]{3,2,1,0:T(8,128)S(1)}, u32[]{:S(2)}, u32[]{:S(2)}) %collective-permute-start.26) | collective-permute-done | bytes 524320 | tf_op jit(solution)/shard_map/ppermute | solution.py:435
  80.0 1.9 %short_dims.8 = (f32[4,8,16,128]{3,2,1,0:T(8,128)S(1)}, f32[4,8,16,128]{3,2,1,0:T(8,128)S(1)}) custom-call(bf16[64,256]{1,0:T(8,128)(2,1)S(1)} %get-tuple-element.93.kron_hi, bf16[64,256]{1,0:T(8,128)(2,1)S(1)} %get-tuple-element.136.kron_lo, bf16[8,256,256]{2,1,0:T(8,128)(2,1)S(1)} %get-tuple-element.64.right3, f32[16,64,128]{2,1,0:T(8,128)S(1)} %bitcast.33, ...), custom_call_target="tpu_custom_call" | custom-call | flops 1000000 | bytes 10000 | tf_op jit(solution)/shard_map/short_dims/pallas_call | solution.py:453
  82.6 1.5 %collective-permute-start.24 = (f32[4,8,16,128]{3,2,1,0:T(8,128)S(1)}, f32[4,8,16,128]{3,2,1,0:T(8,128)S(1)}, u32[]{:S(2)}, u32[]{:S(2)}) collective-permute-start(f32[4,8,16,128]{3,2,1,0:T(8,128)S(1)} %get-tuple-element.91), channel_id=1, source_target_pairs={{0,1},{1,0},{2,3},{3,2},{4,5},{5,4},{6,7},{7,6},{8,9},{9,8},{10,11... | collective-permute-start | bytes 786440 | tf_op jit(solution)/shard_map/ppermute | solution.py:499
  84.1 1.9 %short_dims.9 = (f32[4,8,16,128]{3,2,1,0:T(8,128)S(1)}, f32[4,8,16,128]{3,2,1,0:T(8,128)S(1)}) custom-call(bf16[64,256]{1,0:T(8,128)(2,1)S(1)} %get-tuple-element.99.kron_hi, bf16[64,256]{1,0:T(8,128)(2,1)S(1)} %get-tuple-element.135.kron_lo, bf16[8,256,256]{2,1,0:T(8,128)(2,1)S(1)} %get-tuple-element.64.right3, f32[16,64,128]{2,1,0:T(8,128)S(1)} %bitcast.34, ...), custom_call_target="tpu_custom_call" | custom-call | flops 1000000 | bytes 10000 | tf_op jit(solution)/shard_map/short_dims/pallas_call | solution.py:453
  86.0 4.5 %collective-permute-done.31.refs_7_ = f32[4,8,16,128]{3,2,1,0:T(8,128)S(1)} collective-permute-done((f32[4,8,16,128]{3,2,1,0:T(8,128)S(1)}, f32[4,8,16,128]{3,2,1,0:T(8,128)S(1)}, u32[]{:S(2)}, u32[]{:S(2)}) %collective-permute-start.31) | collective-permute-done | bytes 262176 | tf_op jit(solution)/shard_map/ppermute | solution.py:519
  92.4 1.6 %collective-permute-start.35 = (f32[4,128,128]{2,1,0:T(8,128)S(1)}, f32[4,128,128]{2,1,0:T(8,128)S(1)}, u32[]{:S(2)}, u32[]{:S(2)}) collective-permute-start(f32[4,128,128]{2,1,0:T(8,128)S(1)} %get-tuple-element.109.mine), channel_id=1, source_target_pairs={{0,1},{1,0},{2,3},{3,2},{4,5},{5,4},{6,7},{7,6},{8,9},{9,8},{10,11... | collective-permute-start | bytes 786440 | tf_op jit(solution)/shard_map/ppermute | solution.py:551
  95.8 2.4 %collective-permute-done.32.refs_7_ = f32[4,8,16,128]{3,2,1,0:T(8,128)S(1)} collective-permute-done((f32[4,8,16,128]{3,2,1,0:T(8,128)S(1)}, f32[4,8,16,128]{3,2,1,0:T(8,128)S(1)}, u32[]{:S(2)}, u32[]{:S(2)}) %collective-permute-start.32) | collective-permute-done | bytes 262176 | tf_op jit(solution)/shard_map/ppermute | solution.py:519
  99.5 1.6 %collective-permute-start.34 = (f32[4,128,128]{2,1,0:T(8,128)S(1)}, f32[4,128,128]{2,1,0:T(8,128)S(1)}, u32[]{:S(2)}, u32[]{:S(2)}) collective-permute-start(f32[4,128,128]{2,1,0:T(8,128)S(1)} %get-tuple-element.106.mine), channel_id=1, source_target_pairs={{0,1},{1,0},{2,3},{3,2},{4,5},{5,4},{6,7},{7,6},{8,9},{9,8},{10,11... | collective-permute-start | bytes 786440 | tf_op jit(solution)/shard_map/ppermute | solution.py:551
  101.0 1.3 %third_dim.4 = (f32[4,4,128,128]{3,2,1,0:T(8,128)S(1)}, f32[4,128,128]{2,1,0:T(8,128)S(1)}) custom-call(s32[44]{0:T(128)S(1)} %concatenate.34.meta, f32[8,16]{1,0:T(8,128)S(1)} %copy-done, f32[8,16]{1,0:T(8,128)S(1)} %copy-done.1, bf16[4,256,256]{2,1,0:T(8,128)(2,1)S(1)} %get-tuple-element.60.left2, f32[4,128,128]{2,1,0:T(8,128)S(1)} %get-tuple-element.61.util23, ...), custom_call_target="tpu_custom_call" | custom-call | flops 1000000000 | bytes 5000000 | tf_op jit(solution)/shard_map/third_dim/pallas_call | solution.py:536
  102.9 4.4 %collective-permute-done.36.other = f32[4,128,128]{2,1,0:T(8,128)S(1)} collective-permute-done((f32[4,128,128]{2,1,0:T(8,128)S(1)}, f32[4,128,128]{2,1,0:T(8,128)S(1)}, u32[]{:S(2)}, u32[]{:S(2)}) %collective-permute-start.36) | collective-permute-done | bytes 262176 | tf_op jit(solution)/shard_map/ppermute | solution.py:551
  109.3 3.5 %collective-permute-done.34.other = f32[4,128,128]{2,1,0:T(8,128)S(1)} collective-permute-done((f32[4,128,128]{2,1,0:T(8,128)S(1)}, f32[4,128,128]{2,1,0:T(8,128)S(1)}, u32[]{:S(2)}, u32[]{:S(2)}) %collective-permute-start.34) | collective-permute-done | bytes 262176 | tf_op jit(solution)/shard_map/ppermute | solution.py:551
  113.9 2.8 %collective-permute-done.33.other = f32[4,128,128]{2,1,0:T(8,128)S(1)} collective-permute-done((f32[4,128,128]{2,1,0:T(8,128)S(1)}, f32[4,128,128]{2,1,0:T(8,128)S(1)}, u32[]{:S(2)}, u32[]{:S(2)}) %collective-permute-start.33) | collective-permute-done | bytes 262176 | tf_op jit(solution)/shard_map/ppermute | solution.py:551
  (95 shorter events, 25.6 us)
Async XLA Ops:
  2.0 15.3 %collective-permute-start = (f32[2,8,16,128]{3,2,1,0:T(8,128)S(1)}, f32[2,8,16,128]{3,2,1,0:T(8,128)S(1)}, u32[]{:S(2)}, u32[]{:S(2)}) collective-permute-start(f32[2,8,16,128]{3,2,1,0:T(8,128)S(1)} %get-tuple-element.123), channel_id=1, source_target_pairs={{0,8},{4,12},{8,0},{12,4},{16,24},{20,28},{24,16},{28,20},{1,9},{5... | collective-permute-start | bytes 393224 | tf_op jit(solution)/shard_map/ppermute | solution.py:411
  5.1 12.9 %collective-permute-start.1 = (f32[2,8,16,128]{3,2,1,0:T(8,128)S(1)}, f32[2,8,16,128]{3,2,1,0:T(8,128)S(1)}, u32[]{:S(2)}, u32[]{:S(2)}) collective-permute-start(f32[2,8,16,128]{3,2,1,0:T(8,128)S(1)} %get-tuple-element.123), channel_id=1, source_target_pairs={{0,16},{4,20},{8,24},{12,28},{16,0},{20,4},{24,8},{28,12},{1,17},{... | collective-permute-start | bytes 393224 | tf_op jit(solution)/shard_map/ppermute | solution.py:411
  7.7 10.3 %collective-permute-start.2 = (f32[2,8,16,128]{3,2,1,0:T(8,128)S(1)}, f32[2,8,16,128]{3,2,1,0:T(8,128)S(1)}, u32[]{:S(2)}, u32[]{:S(2)}) collective-permute-start(f32[2,8,16,128]{3,2,1,0:T(8,128)S(1)} %get-tuple-element.123), channel_id=1, source_target_pairs={{0,24},{4,28},{8,16},{12,20},{16,8},{20,12},{24,0},{28,4},{1,25},{... | collective-permute-start | bytes 393224 | tf_op jit(solution)/shard_map/ppermute | solution.py:411
  8.9 14.1 %collective-permute-start.5 = (f32[2,8,64,128]{3,2,1,0:T(8,128)S(1)}, f32[2,8,64,128]{3,2,1,0:T(8,128)S(1)}, u32[]{:S(2)}, u32[]{:S(2)}) collective-permute-start(f32[2,8,64,128]{3,2,1,0:T(8,128)S(1)} %get-tuple-element.125), channel_id=1, source_target_pairs={{0,2},{2,0},{1,3},{3,1},{4,6},{6,4},{5,7},{7,5},{8,10},{10,8},{9,1... | collective-permute-start | bytes 1572872 | tf_op jit(solution)/shard_map/ppermute | solution.py:412
  11.7 10.4 %collective-permute-start.9 = (f32[2,8,32,128]{3,2,1,0:T(8,128)S(1)}, f32[2,8,32,128]{3,2,1,0:T(8,128)S(1)}, u32[]{:S(2)}, u32[]{:S(2)}) collective-permute-start(f32[2,8,32,128]{3,2,1,0:T(8,128)S(1)} %constant_dynamic-slice_fusion.2), channel_id=1, source_target_pairs={{0,8},{4,12},{8,0},{12,4},{16,24},{20,28},{24,16},{28,20},{1,9},{5... | collective-permute-start | bytes 786440 | tf_op jit(solution)/shard_map/ppermute | solution.py:413
  18.1 8.8 %collective-permute-start.3 = (f32[6,8,16,128]{3,2,1,0:T(8,128)S(1)}, f32[6,8,16,128]{3,2,1,0:T(8,128)S(1)}, u32[]{:S(2)}, u32[]{:S(2)}) collective-permute-start(f32[6,8,16,128]{3,2,1,0:T(8,128)S(1)} %constant_dynamic-update-slice_fusion), channel_id=1, source_target_pairs={{0,4},{4,0},{8,12},{12,8},{16,20},{20,16},{24,28},{28,24},{1,5},{5... | collective-permute-start | bytes 1179656 | tf_op jit(solution)/shard_map/ppermute | solution.py:443
  18.2 12.3 %collective-permute-start.7 = (f32[6,8,16,128]{3,2,1,0:T(8,128)S(1)}, f32[6,8,16,128]{3,2,1,0:T(8,128)S(1)}, u32[]{:S(2)}, u32[]{:S(2)}) collective-permute-start(f32[6,8,16,128]{3,2,1,0:T(8,128)S(1)} %constant_dynamic-update-slice_fusion), channel_id=1, source_target_pairs={{0,2},{2,0},{1,3},{3,1},{4,6},{6,4},{5,7},{7,5},{8,10},{10,8},{9,1... | collective-permute-start | bytes 1179656 | tf_op jit(solution)/shard_map/ppermute | solution.py:444
  22.1 14.0 %collective-permute-start.10 = (f32[4,8,16,128]{3,2,1,0:T(8,128)S(1)}, f32[4,8,16,128]{3,2,1,0:T(8,128)S(1)}, u32[]{:S(2)}, u32[]{:S(2)}) collective-permute-start(f32[4,8,16,128]{3,2,1,0:T(8,128)S(1)} %pad_maximum_fusion.5), channel_id=1, source_target_pairs={{0,16},{4,20},{8,24},{12,28},{16,0},{20,4},{24,8},{28,12},{1,17},{... | collective-permute-start | bytes 786440 | tf_op jit(solution)/shard_map/ppermute | solution.py:424
  23.0 13.3 %collective-permute-start.11 = (f32[4,8,16,128]{3,2,1,0:T(8,128)S(1)}, f32[4,8,16,128]{3,2,1,0:T(8,128)S(1)}, u32[]{:S(2)}, u32[]{:S(2)}) collective-permute-start(f32[4,8,16,128]{3,2,1,0:T(8,128)S(1)} %pad_maximum_fusion.6), channel_id=1, source_target_pairs={{0,8},{4,12},{8,0},{12,4},{16,24},{20,28},{24,16},{28,20},{1,9},{5... | collective-permute-start | bytes 786440 | tf_op jit(solution)/shard_map/ppermute | solution.py:445
  26.9 10.0 %collective-permute-start.4 = (f32[2,8,64,128]{3,2,1,0:T(8,128)S(1)}, f32[2,8,64,128]{3,2,1,0:T(8,128)S(1)}, u32[]{:S(2)}, u32[]{:S(2)}) collective-permute-start(f32[2,8,64,128]{3,2,1,0:T(8,128)S(1)} %get-tuple-element.71), channel_id=1, source_target_pairs={{0,4},{4,0},{8,12},{12,8},{16,20},{20,16},{24,28},{28,24},{1,5},{5... | collective-permute-start | bytes 1572872 | tf_op jit(solution)/shard_map/ppermute | solution.py:448
  27.0 10.4 %collective-permute-start.6 = (f32[2,8,64,128]{3,2,1,0:T(8,128)S(1)}, f32[2,8,64,128]{3,2,1,0:T(8,128)S(1)}, u32[]{:S(2)}, u32[]{:S(2)}) collective-permute-start(f32[2,8,64,128]{3,2,1,0:T(8,128)S(1)} %collective-permute-done.5), channel_id=1, source_target_pairs={{0,4},{4,0},{8,12},{12,8},{16,20},{20,16},{24,28},{28,24},{1,5},{5... | collective-permute-start | bytes 1572872 | tf_op jit(solution)/shard_map/ppermute | solution.py:449
  30.5 6.4 %collective-permute-start.8 = (f32[6,8,16,128]{3,2,1,0:T(8,128)S(1)}, f32[6,8,16,128]{3,2,1,0:T(8,128)S(1)}, u32[]{:S(2)}, u32[]{:S(2)}) collective-permute-start(f32[6,8,16,128]{3,2,1,0:T(8,128)S(1)} %collective-permute-done.7), channel_id=1, source_target_pairs={{0,4},{4,0},{8,12},{12,8},{16,20},{20,16},{24,28},{28,24},{1,5},{5... | collective-permute-start | bytes 1179656 | tf_op jit(solution)/shard_map/ppermute | solution.py:485
  36.1 14.1 %collective-permute-start.17 = (f32[4,8,16,128]{3,2,1,0:T(8,128)S(1)}, f32[4,8,16,128]{3,2,1,0:T(8,128)S(1)}, u32[]{:S(2)}, u32[]{:S(2)}) collective-permute-start(f32[4,8,16,128]{3,2,1,0:T(8,128)S(1)} %pad_maximum_fusion.7), channel_id=1, source_target_pairs={{0,16},{4,20},{8,24},{12,28},{16,0},{20,4},{24,8},{28,12},{1,17},{... | collective-permute-start | bytes 786440 | tf_op jit(solution)/shard_map/ppermute | solution.py:424
  36.3 14.0 %collective-permute-start.13 = (f32[6,8,16,128]{3,2,1,0:T(8,128)S(1)}, f32[6,8,16,128]{3,2,1,0:T(8,128)S(1)}, u32[]{:S(2)}, u32[]{:S(2)}) collective-permute-start(f32[6,8,16,128]{3,2,1,0:T(8,128)S(1)} %pad_maximum_fusion.3), channel_id=1, source_target_pairs={{0,2},{2,0},{1,3},{3,1},{4,6},{6,4},{5,7},{7,5},{8,10},{10,8},{9,1... | collective-permute-start | bytes 1179656 | tf_op jit(solution)/shard_map/ppermute | solution.py:479
  36.8 14.2 %collective-permute-start.14 = (f32[2,8,16,128]{3,2,1,0:T(8,128)S(1)}, f32[2,8,16,128]{3,2,1,0:T(8,128)S(1)}, u32[]{:S(2)}, u32[]{:S(2)}) collective-permute-start(f32[2,8,16,128]{3,2,1,0:T(8,128)S(1)} %get-tuple-element.134), channel_id=1, source_target_pairs={{0,4},{4,0},{8,12},{12,8},{16,20},{20,16},{24,28},{28,24},{1,5},{5... | collective-permute-start | bytes 393224 | tf_op jit(solution)/shard_map/ppermute | solution.py:470
  36.9 14.2 %collective-permute-start.15 = (f32[2,8,16,128]{3,2,1,0:T(8,128)S(1)}, f32[2,8,16,128]{3,2,1,0:T(8,128)S(1)}, u32[]{:S(2)}, u32[]{:S(2)}) collective-permute-start(f32[2,8,16,128]{3,2,1,0:T(8,128)S(1)} %get-tuple-element.133), channel_id=1, source_target_pairs={{0,4},{4,0},{8,12},{12,8},{16,20},{20,16},{24,28},{28,24},{1,5},{5... | collective-permute-start | bytes 393224 | tf_op jit(solution)/shard_map/ppermute | solution.py:470
  39.7 15.9 %collective-permute-start.21 = (f32[4,16,16,128]{3,2,1,0:T(8,128)S(1)}, f32[4,16,16,128]{3,2,1,0:T(8,128)S(1)}, u32[]{:S(2)}, u32[]{:S(2)}) collective-permute-start(f32[4,16,16,128]{3,2,1,0:T(8,128)S(1)} %get-tuple-element.85), channel_id=1, source_target_pairs={{0,1},{1,0},{2,3},{3,2},{4,5},{5,4},{6,7},{7,6},{8,9},{9,8},{10,11... | collective-permute-start | bytes 1572872 | tf_op jit(solution)/shard_map/ppermute | solution.py:499
  50.3 12.4 %collective-permute-start.25 = (f32[8,8,16,128]{3,2,1,0:T(8,128)S(1)}, f32[8,8,16,128]{3,2,1,0:T(8,128)S(1)}, u32[]{:S(2)}, u32[]{:S(2)}) collective-permute-start(f32[8,8,16,128]{3,2,1,0:T(8,128)S(1)} %pad_maximum_fusion.2), channel_id=1, source_target_pairs={{8,16},{12,20},{16,8},{20,12},{9,17},{13,21},{17,9},{21,13},{10,18... | collective-permute-start | bytes 1572872 | tf_op jit(solution)/shard_map/ppermute | solution.py:434
  51.0 1.8 %collective-permute-start.12 = (f32[6,8,16,128]{3,2,1,0:T(8,128)S(1)}, f32[6,8,16,128]{3,2,1,0:T(8,128)S(1)}, u32[]{:S(2)}, u32[]{:S(2)}) collective-permute-start(f32[6,8,16,128]{3,2,1,0:T(8,128)S(1)} %pad_maximum_fusion.3), channel_id=1, source_target_pairs={{0,4},{4,0},{8,12},{12,8},{16,20},{20,16},{24,28},{28,24},{1,5},{5... | collective-permute-start | bytes 1179656 | tf_op jit(solution)/shard_map/ppermute | solution.py:478
  51.1 2.3 %collective-permute-start.16 = (f32[6,8,16,128]{3,2,1,0:T(8,128)S(1)}, f32[6,8,16,128]{3,2,1,0:T(8,128)S(1)}, u32[]{:S(2)}, u32[]{:S(2)}) collective-permute-start(f32[6,8,16,128]{3,2,1,0:T(8,128)S(1)} %collective-permute-done.13), channel_id=1, source_target_pairs={{0,4},{4,0},{8,12},{12,8},{16,20},{20,16},{24,28},{28,24},{1,5},{5... | collective-permute-start | bytes 1179656 | tf_op jit(solution)/shard_map/ppermute | solution.py:485
  51.6 11.1 %collective-permute-start.19 = (f32[6,8,16,128]{3,2,1,0:T(8,128)S(1)}, f32[6,8,16,128]{3,2,1,0:T(8,128)S(1)}, u32[]{:S(2)}, u32[]{:S(2)}) collective-permute-start(f32[6,8,16,128]{3,2,1,0:T(8,128)S(1)} %pad_maximum_fusion.4), channel_id=1, source_target_pairs={{0,2},{2,0},{1,3},{3,1},{4,6},{6,4},{5,7},{7,5},{8,10},{10,8},{9,1... | collective-permute-start | bytes 1179656 | tf_op jit(solution)/shard_map/ppermute | solution.py:479
  55.6 14.0 %collective-permute-start.22 = (f32[4,16,16,128]{3,2,1,0:T(8,128)S(1)}, f32[4,16,16,128]{3,2,1,0:T(8,128)S(1)}, u32[]{:S(2)}, u32[]{:S(2)}) collective-permute-start(f32[4,16,16,128]{3,2,1,0:T(8,128)S(1)} %get-tuple-element.87), channel_id=1, source_target_pairs={{0,1},{1,0},{2,3},{3,2},{4,5},{5,4},{6,7},{7,6},{8,9},{9,8},{10,11... | collective-permute-start | bytes 1572872 | tf_op jit(solution)/shard_map/ppermute | solution.py:499
  62.7 15.0 %collective-permute-start.26 = (f32[8,8,16,128]{3,2,1,0:T(8,128)S(1)}, f32[8,8,16,128]{3,2,1,0:T(8,128)S(1)}, u32[]{:S(2)}, u32[]{:S(2)}) collective-permute-start(f32[8,8,16,128]{3,2,1,0:T(8,128)S(1)} %collective-permute-done.25), channel_id=1, source_target_pairs={{8,0},{12,4},{16,24},{20,28},{9,1},{13,5},{17,25},{21,29},{10,2},{... | collective-permute-start | bytes 1572872 | tf_op jit(solution)/shard_map/ppermute | solution.py:435
  64.2 2.3 %collective-permute-start.20 = (f32[6,8,16,128]{3,2,1,0:T(8,128)S(1)}, f32[6,8,16,128]{3,2,1,0:T(8,128)S(1)}, u32[]{:S(2)}, u32[]{:S(2)}) collective-permute-start(f32[6,8,16,128]{3,2,1,0:T(8,128)S(1)} %collective-permute-done.19), channel_id=1, source_target_pairs={{0,4},{4,0},{8,12},{12,8},{16,20},{20,16},{24,28},{28,24},{1,5},{5... | collective-permute-start | bytes 1179656 | tf_op jit(solution)/shard_map/ppermute | solution.py:485
  69.7 9.3 %collective-permute-start.23 = (f32[4,8,16,128]{3,2,1,0:T(8,128)S(1)}, f32[4,8,16,128]{3,2,1,0:T(8,128)S(1)}, u32[]{:S(2)}, u32[]{:S(2)}) collective-permute-start(f32[4,8,16,128]{3,2,1,0:T(8,128)S(1)} %get-tuple-element.90), channel_id=1, source_target_pairs={{0,1},{1,0},{2,3},{3,2},{4,5},{5,4},{6,7},{7,6},{8,9},{9,8},{10,11... | collective-permute-start | bytes 786440 | tf_op jit(solution)/shard_map/ppermute | solution.py:499
  81.9 8.6 %collective-permute-start.31 = (f32[4,8,16,128]{3,2,1,0:T(8,128)S(1)}, f32[4,8,16,128]{3,2,1,0:T(8,128)S(1)}, u32[]{:S(2)}, u32[]{:S(2)}) collective-permute-start(f32[4,8,16,128]{3,2,1,0:T(8,128)S(1)} %get-tuple-element.98), channel_id=1, source_target_pairs={{0,2},{2,0},{1,3},{3,1},{4,6},{6,4},{5,7},{7,5},{8,10},{10,8},{9,1... | collective-permute-start | bytes 786440 | tf_op jit(solution)/shard_map/ppermute | solution.py:519
  82.6 13.2 %collective-permute-start.24 = (f32[4,8,16,128]{3,2,1,0:T(8,128)S(1)}, f32[4,8,16,128]{3,2,1,0:T(8,128)S(1)}, u32[]{:S(2)}, u32[]{:S(2)}) collective-permute-start(f32[4,8,16,128]{3,2,1,0:T(8,128)S(1)} %get-tuple-element.91), channel_id=1, source_target_pairs={{0,1},{1,0},{2,3},{3,2},{4,5},{5,4},{6,7},{7,6},{8,9},{9,8},{10,11... | collective-permute-start | bytes 786440 | tf_op jit(solution)/shard_map/ppermute | solution.py:499
  90.5 7.7 %collective-permute-start.32 = (f32[4,8,16,128]{3,2,1,0:T(8,128)S(1)}, f32[4,8,16,128]{3,2,1,0:T(8,128)S(1)}, u32[]{:S(2)}, u32[]{:S(2)}) collective-permute-start(f32[4,8,16,128]{3,2,1,0:T(8,128)S(1)} %get-tuple-element.102), channel_id=1, source_target_pairs={{0,2},{2,0},{1,3},{3,1},{4,6},{6,4},{5,7},{7,5},{8,10},{10,8},{9,1... | collective-permute-start | bytes 786440 | tf_op jit(solution)/shard_map/ppermute | solution.py:519
  92.4 16.0 %collective-permute-start.35 = (f32[4,128,128]{2,1,0:T(8,128)S(1)}, f32[4,128,128]{2,1,0:T(8,128)S(1)}, u32[]{:S(2)}, u32[]{:S(2)}) collective-permute-start(f32[4,128,128]{2,1,0:T(8,128)S(1)} %get-tuple-element.109.mine), channel_id=1, source_target_pairs={{0,1},{1,0},{2,3},{3,2},{4,5},{5,4},{6,7},{7,6},{8,9},{9,8},{10,11... | collective-permute-start | bytes 786440 | tf_op jit(solution)/shard_map/ppermute | solution.py:551
  95.2 12.1 %collective-permute-start.36 = (f32[4,128,128]{2,1,0:T(8,128)S(1)}, f32[4,128,128]{2,1,0:T(8,128)S(1)}, u32[]{:S(2)}, u32[]{:S(2)}) collective-permute-start(f32[4,128,128]{2,1,0:T(8,128)S(1)} %get-tuple-element.111.mine), channel_id=1, source_target_pairs={{0,1},{1,0},{2,3},{3,2},{4,5},{5,4},{6,7},{7,6},{8,9},{9,8},{10,11... | collective-permute-start | bytes 786440 | tf_op jit(solution)/shard_map/ppermute | solution.py:551
  99.5 13.4 %collective-permute-start.34 = (f32[4,128,128]{2,1,0:T(8,128)S(1)}, f32[4,128,128]{2,1,0:T(8,128)S(1)}, u32[]{:S(2)}, u32[]{:S(2)}) collective-permute-start(f32[4,128,128]{2,1,0:T(8,128)S(1)} %get-tuple-element.106.mine), channel_id=1, source_target_pairs={{0,1},{1,0},{2,3},{3,2},{4,5},{5,4},{6,7},{7,6},{8,9},{9,8},{10,11... | collective-permute-start | bytes 786440 | tf_op jit(solution)/shard_map/ppermute | solution.py:551
  102.3 14.4 %collective-permute-start.33 = (f32[4,128,128]{2,1,0:T(8,128)S(1)}, f32[4,128,128]{2,1,0:T(8,128)S(1)}, u32[]{:S(2)}, u32[]{:S(2)}) collective-permute-start(f32[4,128,128]{2,1,0:T(8,128)S(1)} %get-tuple-element.104.mine), channel_id=1, source_target_pairs={{0,1},{1,0},{2,3},{3,2},{4,5},{5,4},{6,7},{7,6},{8,9},{9,8},{10,11... | collective-permute-start | bytes 786440 | tf_op jit(solution)/shard_map/ppermute | solution.py:551
  (12 other events, 73.5 us)

commit v2 on v1

--- a/solution.py
+++ b/solution.py
@@ -522,19 +522,19 @@
     parts = [(keep, None) for keep in kept] + [(ones[0], None) for ones in sent[:-1]]
     parts += [(sent[-1][0], sent[-1]), (side_keep[0], side_keep), (side_got[0], side_got)]
     by_row = []
-    units = [(row, piece) for row in range(rows0) for piece in range(2)]
-    unit1 = rows1 // 2
+    units = [(row, piece) for row in range(rows0) for piece in range(4)]
+    unit1 = rows1 // 4
     for row, piece in units:
         arrays = [cut[row] if cut else one for one, cut in parts]
         specs = [
             pl.BlockSpec(
                 (per_group, unit1) + one.shape[2:],
-                lambda i, block=piece if cut else 2 * row + piece: (0, block, 0, 0),
+                lambda i, block=piece if cut else 4 * row + piece: (0, block, 0, 0),
             )
             for one, (_, cut) in zip(arrays, parts)
         ]
         scores, local = pl.pallas_call(
-            functools.partial(third_dim_kernel, len(parts), rows0, row, 2, piece),
+            functools.partial(third_dim_kernel, len(parts), rows0, row, 4, piece),
             grid=(1,),
             out_shape=(
                 jax.ShapeDtypeStruct((per_group, unit1, len2, len3), F32),

time: 118 us -> 119 us (level)
  waiting for transfers between devices: 55.8 us -> 43.4 us
  starting transfers between devices: 31 us -> 37.9 us
  Pallas kernels: 25.9 us -> 31.9 us
    ppermute x4 -> x8, waiting for transfers between devices: 10.7 us -> 2.81 us  [gather_body(): by_row.append((scores, local, lax.ppermute(local, 'act', act_flip)))]
    ppermute x4 -> x8, starting transfers between devices: 4.32 us -> 8.56 us  [gather_body(): by_row.append((scores, local, lax.ppermute(local, 'act', act_flip)))]
    ppermute x2, waiting for transfers between devices: 14.7 us -> 10.9 us  [doubled(): more = lax.ppermute(grown, 'wide', across(bit))]
    pallas_call x4 -> x8, Pallas kernels: 5.01 us -> 8.59 us  [gather_body(): pl.pallas_call(functools.partial(third_dim_kernel, len(parts), rows0, row...]
    ppermute x2, waiting for transfers between devices: 6.93 us -> 3.81 us  [gather_body(): lax.ppermute(after(give, *side_got[-1:]), 'narrow', narrow_flip)]
    ppermute x1, waiting for transfers between devices: 0.01 us -> 2.78 us  [gather_body(): around = lax.ppermute(to_narrow, 'narrow', narrow_flip)]
    pallas_call x4 -> x8, Pallas kernels: 4.14 us -> 6.54 us  [gather_body(): pl.pallas_call(choice_kernel, grid=(1,), out_shape=(jax.ShapeDtypeStruct(...]
    ppermute x2, starting transfers between devices: 0.52 us -> 2.73 us  [gather_body(): moved.append(lax.ppermute(after(far, moved[-1]), 'narrow', narrow_flip))]
  transfers between devices with their start and end apart: 37 -> 41, of which waited for: 22 -> 21; matrix products, arithmetic and copies ran while one was open for 2% -> 2% of each run, Pallas kernels for 19% -> 25%
where the time goes in v2:
time: 119 us; the launch traced here: 118 us
  waiting for transfers between devices  43.4 us (36%)
  starting transfers between devices  37.9 us (32%)
  Pallas kernels  31.9 us (27%)
  local copies, waits for them, and re-layouts  3.74 us (3%)
    ppermute x2, waiting for transfers between devices, doubled(): more = lax.ppermute(grown, 'wide', across(bit))  10.9 us
    pallas_call x5, Pallas kernels, contract(): pl.pallas_call(functools.partial(short_dims_kernel, views, routes), out_s...  10.7 us
    pallas_call x8, Pallas kernels, gather_body(): pl.pallas_call(functools.partial(third_dim_kernel, len(parts), rows0, row...  8.59 us
    ppermute x8, starting transfers between devices, gather_body(): by_row.append((scores, local, lax.ppermute(local, 'act', act_flip)))  8.56 us
    ppermute x1, waiting for transfers between devices, by_line(): passed = lax.ppermute(after(came, moved[-1]), 'wide', outward)  6.71 us
    pallas_call x8, Pallas kernels, gather_body(): pl.pallas_call(choice_kernel, grid=(1,), out_shape=(jax.ShapeDtypeStruct(...  6.54 us
    ppermute x3, starting transfers between devices, gather_body(): lax.ppermute(chunks[0], 'wide', across(far))  5.76 us
    ppermute x4, starting transfers between devices, gather_body(): sent[-1].append(lax.ppermute(after(one, *before), 'act', act_flip))  5.75 us
  transfers between devices with their start and end apart: 41, of which 21 were waited for; matrix products, arithmetic and copies ran while one was open for 2% of the time, Pallas kernels for 25%

profile of v2, /device:TPU:0, one launch (start us, length us, event | category | flops | bytes accessed | tf_op | source)
XLA Modules:
  0.0 118.4 jit_solution(18254384858937125441)
XLA Ops:
  0.7 1.4 %constant_dynamic-slice_fusion = (f32[2,8,16,128]{3,2,1,0:T(8,128)S(1)}, f32[2,8,16,128]{3,2,1,0:T(8,128)S(1)}, f32[2,8,16,128]{3,2,1,0:T(8,128)S(1)}, f32[2,8,16,128]{3,2,1,0:T(8,128)S(1)}, f32[2,8,16,128]{3,2,1,0:T(8,128)S(1)}) fusion(f32[2,8,128,128]{3,2,1,0:T(8,128)} %param.8, s32[]{:T(128)S(6)} %select_n.47, s32[]{:T(128)S(6)} %select_n.46, ...), kind=kLoop, calls=%fused_computation.13 | loop fusion | bytes 1310740 | tf_op jit(solution)/shard_map/dynamic_slice | solution.py:345
  2.0 5.1 %collective-permute-start.2 = (f32[2,8,16,128]{3,2,1,0:T(8,128)S(1)}, f32[2,8,16,128]{3,2,1,0:T(8,128)S(1)}, u32[]{:S(2)}, u32[]{:S(2)}) collective-permute-start(f32[2,8,16,128]{3,2,1,0:T(8,128)S(1)} %get-tuple-element.155), channel_id=1, source_target_pairs={{0,24},{4,28},{8,16},{12,20},{16,8},{20,12},{24,0},{28,4},{1,25},{... | collective-permute-start | bytes 393224 | tf_op jit(solution)/shard_map/ppermute | solution.py:411
  8.8 1.5 %collective-permute-start.9 = (f32[2,8,32,128]{3,2,1,0:T(8,128)S(1)}, f32[2,8,32,128]{3,2,1,0:T(8,128)S(1)}, u32[]{:S(2)}, u32[]{:S(2)}) collective-permute-start(f32[2,8,32,128]{3,2,1,0:T(8,128)S(1)} %constant_dynamic-slice_fusion.2), channel_id=1, source_target_pairs={{0,8},{4,12},{8,0},{12,4},{16,24},{20,28},{24,16},{28,20},{1,9},{5... | collective-permute-start | bytes 786440 | tf_op jit(solution)/shard_map/ppermute | solution.py:413
  11.4 1.6 %collective-permute-start.5 = (f32[2,8,64,128]{3,2,1,0:T(8,128)S(1)}, f32[2,8,64,128]{3,2,1,0:T(8,128)S(1)}, u32[]{:S(2)}, u32[]{:S(2)}) collective-permute-start(f32[2,8,64,128]{3,2,1,0:T(8,128)S(1)} %get-tuple-element.157), channel_id=1, source_target_pairs={{0,2},{2,0},{1,3},{3,1},{4,6},{6,4},{5,7},{7,5},{8,10},{10,8},{9,1... | collective-permute-start | bytes 1572872 | tf_op jit(solution)/shard_map/ppermute | solution.py:412
  13.2 4.7 %prepare.1 = (bf16[128,256]{1,0:T(8,128)(2,1)S(1)}, bf16[128,256]{1,0:T(8,128)(2,1)S(1)}, bf16[128,256]{1,0:T(8,128)(2,1)S(1)}, bf16[128,256]{1,0:T(8,128)(2,1)S(1)}, bf16[8,256,256]{2,1,0:T(8,128)(2,1)S(1)}) custom-call(s32[44]{0:T(128)S(1)} %concatenate.34.meta, f32[8,4,256]{2,1,0:T(4,128)S(1)} %pad.4.weights), custom_call_target="tpu_custom_call" | custom-call | flops 1000000000 | bytes 4000000 | tf_op jit(solution)/shard_map/prepare/pallas_call | solution.py:362
  18.4 1.6 %collective-permute-start.7 = (f32[6,8,16,128]{3,2,1,0:T(8,128)S(1)}, f32[6,8,16,128]{3,2,1,0:T(8,128)S(1)}, u32[]{:S(2)}, u32[]{:S(2)}) collective-permute-start(f32[6,8,16,128]{3,2,1,0:T(8,128)S(1)} %constant_dynamic-update-slice_fusion), channel_id=1, source_target_pairs={{0,2},{2,0},{1,3},{3,1},{4,6},{6,4},{5,7},{7,5},{8,10},{10,8},{9,1... | collective-permute-start | bytes 1179656 | tf_op jit(solution)/shard_map/ppermute | solution.py:444
  20.0 2.0 %collective-permute-done.9 = f32[2,8,32,128]{3,2,1,0:T(8,128)S(1)} collective-permute-done((f32[2,8,32,128]{3,2,1,0:T(8,128)S(1)}, f32[2,8,32,128]{3,2,1,0:T(8,128)S(1)}, u32[]{:S(2)}, u32[]{:S(2)}) %collective-permute-start.9) | collective-permute-done | bytes 262176 | tf_op jit(solution)/shard_map/ppermute | solution.py:413
  22.0 1.5 %collective-permute-start.10 = (f32[4,8,16,128]{3,2,1,0:T(8,128)S(1)}, f32[4,8,16,128]{3,2,1,0:T(8,128)S(1)}, u32[]{:S(2)}, u32[]{:S(2)}) collective-permute-start(f32[4,8,16,128]{3,2,1,0:T(8,128)S(1)} %pad_maximum_fusion.5), channel_id=1, source_target_pairs={{0,16},{4,20},{8,24},{12,28},{16,0},{20,4},{24,8},{28,12},{1,17},{... | collective-permute-start | bytes 786440 | tf_op jit(solution)/shard_map/ppermute | solution.py:424
  23.6 2.8 %collective-permute-done.5 = f32[2,8,64,128]{3,2,1,0:T(8,128)S(1)} collective-permute-done((f32[2,8,64,128]{3,2,1,0:T(8,128)S(1)}, f32[2,8,64,128]{3,2,1,0:T(8,128)S(1)}, u32[]{:S(2)}, u32[]{:S(2)}) %collective-permute-start.5) | collective-permute-done | bytes 524320 | tf_op jit(solution)/shard_map/ppermute | solution.py:412
  27.1 1.3 %prepare_third.1 = (bf16[4,256,256]{2,1,0:T(8,128)(2,1)S(1)}, f32[4,128,128]{2,1,0:T(8,128)S(1)}) custom-call(s32[44]{0:T(128)S(1)} %concatenate.34.meta, f32[8,4,256]{2,1,0:T(4,128)S(1)} %pad.4.weights, f32[8,128]{1,0:T(8,128)S(1)} %copy-done.2, f32[8,128]{1,0:T(8,128)S(1)} %copy-done.3), custom_call_target="tpu_custom_call" | custom-call | flops 1000000000 | bytes 4000000 | tf_op jit(solution)/shard_map/prepare_third/pallas_call | solution.py:382
  29.0 3.7 %collective-permute-done.7 = f32[6,8,16,128]{3,2,1,0:T(8,128)S(1)} collective-permute-done((f32[6,8,16,128]{3,2,1,0:T(8,128)S(1)}, f32[6,8,16,128]{3,2,1,0:T(8,128)S(1)}, u32[]{:S(2)}, u32[]{:S(2)}) %collective-permute-start.7) | collective-permute-done | bytes 393248 | tf_op jit(solution)/shard_map/ppermute | solution.py:444
  32.7 3.9 %collective-permute-done.10 = f32[4,8,16,128]{3,2,1,0:T(8,128)S(1)} collective-permute-done((f32[4,8,16,128]{3,2,1,0:T(8,128)S(1)}, f32[4,8,16,128]{3,2,1,0:T(8,128)S(1)}, u32[]{:S(2)}, u32[]{:S(2)}) %collective-permute-start.10) | collective-permute-done | bytes 262176 | tf_op jit(solution)/shard_map/ppermute | solution.py:424
  37.2 1.4 %collective-permute-start.13 = (f32[6,8,16,128]{3,2,1,0:T(8,128)S(1)}, f32[6,8,16,128]{3,2,1,0:T(8,128)S(1)}, u32[]{:S(2)}, u32[]{:S(2)}) collective-permute-start(f32[6,8,16,128]{3,2,1,0:T(8,128)S(1)} %pad_maximum_fusion.3), channel_id=1, source_target_pairs={{0,2},{2,0},{1,3},{3,1},{4,6},{6,4},{5,7},{7,5},{8,10},{10,8},{9,1... | collective-permute-start | bytes 1179656 | tf_op jit(solution)/shard_map/ppermute | solution.py:479
  39.3 2.3 %short_dims.5 = (f32[4,16,16,128]{3,2,1,0:T(8,128)S(1)}, f32[4,16,16,128]{3,2,1,0:T(8,128)S(1)}) custom-call(bf16[128,256]{1,0:T(8,128)(2,1)S(1)} %get-tuple-element.78.kron_hi, bf16[128,256]{1,0:T(8,128)(2,1)S(1)} %get-tuple-element.79.kron_lo, bf16[8,256,256]{2,1,0:T(8,128)(2,1)S(1)} %get-tuple-element.80.right3, f32[16,64,128]{2,1,0:T(8,128)S(1)} %bitcast.30, ...), custom_call_target="tpu_custom_call" | custom-call | flops 1000000 | bytes 10000 | tf_op jit(solution)/shard_map/short_dims/pallas_call | solution.py:453
  41.6 1.6 %collective-permute-start.21 = (f32[4,16,16,128]{3,2,1,0:T(8,128)S(1)}, f32[4,16,16,128]{3,2,1,0:T(8,128)S(1)}, u32[]{:S(2)}, u32[]{:S(2)}) collective-permute-start(f32[4,16,16,128]{3,2,1,0:T(8,128)S(1)} %get-tuple-element.101), channel_id=1, source_target_pairs={{0,1},{1,0},{2,3},{3,2},{4,5},{5,4},{6,7},{7,6},{8,9},{9,8},{10,11... | collective-permute-start | bytes 1572872 | tf_op jit(solution)/shard_map/ppermute | solution.py:499
  43.2 7.1 %collective-permute-done.17 = f32[4,8,16,128]{3,2,1,0:T(8,128)S(1)} collective-permute-done((f32[4,8,16,128]{3,2,1,0:T(8,128)S(1)}, f32[4,8,16,128]{3,2,1,0:T(8,128)S(1)}, u32[]{:S(2)}, u32[]{:S(2)}) %collective-permute-start.17) | collective-permute-done | bytes 262176 | tf_op jit(solution)/shard_map/ppermute | solution.py:424
  53.4 2.3 %short_dims.6 = (f32[4,16,16,128]{3,2,1,0:T(8,128)S(1)}, f32[4,16,16,128]{3,2,1,0:T(8,128)S(1)}) custom-call(bf16[128,256]{1,0:T(8,128)(2,1)S(1)} %get-tuple-element.78.kron_hi, bf16[128,256]{1,0:T(8,128)(2,1)S(1)} %get-tuple-element.79.kron_lo, bf16[8,256,256]{2,1,0:T(8,128)(2,1)S(1)} %get-tuple-element.80.right3, f32[16,64,128]{2,1,0:T(8,128)S(1)} %bitcast.31, ...), custom_call_target="tpu_custom_call" | custom-call | flops 1000000 | bytes 10000 | tf_op jit(solution)/shard_map/short_dims/pallas_call | solution.py:453
  55.7 1.4 %collective-permute-start.22 = (f32[4,16,16,128]{3,2,1,0:T(8,128)S(1)}, f32[4,16,16,128]{3,2,1,0:T(8,128)S(1)}, u32[]{:S(2)}, u32[]{:S(2)}) collective-permute-start(f32[4,16,16,128]{3,2,1,0:T(8,128)S(1)} %get-tuple-element.103), channel_id=1, source_target_pairs={{0,1},{1,0},{2,3},{3,2},{4,5},{5,4},{6,7},{7,6},{8,9},{9,8},{10,11... | collective-permute-start | bytes 1572872 | tf_op jit(solution)/shard_map/ppermute | solution.py:499
  57.1 5.6 %collective-permute-done.19 = f32[6,8,16,128]{3,2,1,0:T(8,128)S(1)} collective-permute-done((f32[6,8,16,128]{3,2,1,0:T(8,128)S(1)}, f32[6,8,16,128]{3,2,1,0:T(8,128)S(1)}, u32[]{:S(2)}, u32[]{:S(2)}) %collective-permute-start.19) | collective-permute-done | bytes 393248 | tf_op jit(solution)/shard_map/ppermute | solution.py:479
  62.7 1.5 %collective-permute-start.26 = (f32[8,8,16,128]{3,2,1,0:T(8,128)S(1)}, f32[8,8,16,128]{3,2,1,0:T(8,128)S(1)}, u32[]{:S(2)}, u32[]{:S(2)}) collective-permute-start(f32[8,8,16,128]{3,2,1,0:T(8,128)S(1)} %collective-permute-done.25), channel_id=1, source_target_pairs={{8,0},{12,4},{16,24},{20,28},{9,1},{13,5},{17,25},{21,29},{10,2},{... | collective-permute-start | bytes 1572872 | tf_op jit(solution)/shard_map/ppermute | solution.py:435
  66.5 2.3 %short_dims.7 = (f32[4,16,16,128]{3,2,1,0:T(8,128)S(1)}, f32[4,8,16,128]{3,2,1,0:T(8,128)S(1)}, f32[4,8,16,128]{3,2,1,0:T(8,128)S(1)}) custom-call(bf16[128,256]{1,0:T(8,128)(2,1)S(1)} %get-tuple-element.78.kron_hi, bf16[128,256]{1,0:T(8,128)(2,1)S(1)} %get-tuple-element.79.kron_lo, bf16[8,256,256]{2,1,0:T(8,128)(2,1)S(1)} %get-tuple-element.80.right3, ...), custom_call_target="tpu_custom_call" | custom-call | flops 1000000 | bytes 10000 | tf_op jit(solution)/shard_map/short_dims/pallas_call | solution.py:453
  71.0 6.7 %collective-permute-done.26 = f32[8,8,16,128]{3,2,1,0:T(8,128)S(1)} collective-permute-done((f32[8,8,16,128]{3,2,1,0:T(8,128)S(1)}, f32[8,8,16,128]{3,2,1,0:T(8,128)S(1)}, u32[]{:S(2)}, u32[]{:S(2)}) %collective-permute-start.26) | collective-permute-done | bytes 524320 | tf_op jit(solution)/shard_map/ppermute | solution.py:435
  80.0 1.9 %short_dims.8 = (f32[4,8,16,128]{3,2,1,0:T(8,128)S(1)}, f32[4,8,16,128]{3,2,1,0:T(8,128)S(1)}) custom-call(bf16[64,256]{1,0:T(8,128)(2,1)S(1)} %get-tuple-element.109.kron_hi, bf16[64,256]{1,0:T(8,128)(2,1)S(1)} %get-tuple-element.168.kron_lo, bf16[8,256,256]{2,1,0:T(8,128)(2,1)S(1)} %get-tuple-element.80.right3, f32[16,64,128]{2,1,0:T(8,128)S(1)} %bitcast.33, ...), custom_call_target="tpu_custom_call" | custom-call | flops 1000000 | bytes 10000 | tf_op jit(solution)/shard_map/short_dims/pallas_call | solution.py:453
  81.9 1.4 %collective-permute-start.31 = (f32[4,8,16,128]{3,2,1,0:T(8,128)S(1)}, f32[4,8,16,128]{3,2,1,0:T(8,128)S(1)}, u32[]{:S(2)}, u32[]{:S(2)}) collective-permute-start(f32[4,8,16,128]{3,2,1,0:T(8,128)S(1)} %get-tuple-element.114), channel_id=1, source_target_pairs={{0,2},{2,0},{1,3},{3,1},{4,6},{6,4},{5,7},{7,5},{8,10},{10,8},{9,1... | collective-permute-start | bytes 786440 | tf_op jit(solution)/shard_map/ppermute | solution.py:519
  83.3 1.5 %collective-permute-start.24 = (f32[4,8,16,128]{3,2,1,0:T(8,128)S(1)}, f32[4,8,16,128]{3,2,1,0:T(8,128)S(1)}, u32[]{:S(2)}, u32[]{:S(2)}) collective-permute-start(f32[4,8,16,128]{3,2,1,0:T(8,128)S(1)} %get-tuple-element.107), channel_id=1, source_target_pairs={{0,1},{1,0},{2,3},{3,2},{4,5},{5,4},{6,7},{7,6},{8,9},{9,8},{10,11... | collective-permute-start | bytes 786440 | tf_op jit(solution)/shard_map/ppermute | solution.py:499
  84.8 1.9 %short_dims.9 = (f32[4,8,16,128]{3,2,1,0:T(8,128)S(1)}, f32[4,8,16,128]{3,2,1,0:T(8,128)S(1)}) custom-call(bf16[64,256]{1,0:T(8,128)(2,1)S(1)} %get-tuple-element.115.kron_hi, bf16[64,256]{1,0:T(8,128)(2,1)S(1)} %get-tuple-element.167.kron_lo, bf16[8,256,256]{2,1,0:T(8,128)(2,1)S(1)} %get-tuple-element.80.right3, f32[16,64,128]{2,1,0:T(8,128)S(1)} %bitcast.34, ...), custom_call_target="tpu_custom_call" | custom-call | flops 1000000 | bytes 10000 | tf_op jit(solution)/shard_map/short_dims/pallas_call | solution.py:453
  86.7 3.8 %collective-permute-done.31.refs_7_ = f32[4,8,16,128]{3,2,1,0:T(8,128)S(1)} collective-permute-done((f32[4,8,16,128]{3,2,1,0:T(8,128)S(1)}, f32[4,8,16,128]{3,2,1,0:T(8,128)S(1)}, u32[]{:S(2)}, u32[]{:S(2)}) %collective-permute-start.31) | collective-permute-done | bytes 262176 | tf_op jit(solution)/shard_map/ppermute | solution.py:519
  92.9 1.6 %collective-permute-start.40 = (f32[2,128,128]{2,1,0:T(8,128)S(1)}, f32[2,128,128]{2,1,0:T(8,128)S(1)}, u32[]{:S(2)}, u32[]{:S(2)}) collective-permute-start(f32[2,128,128]{2,1,0:T(8,128)S(1)} %get-tuple-element.135.mine), channel_id=1, source_target_pairs={{0,1},{1,0},{2,3},{3,2},{4,5},{5,4},{6,7},{7,6},{8,9},{9,8},{10,11... | collective-permute-start | bytes 393224 | tf_op jit(solution)/shard_map/ppermute | solution.py:551
  97.2 1.6 %collective-permute-start.38 = (f32[2,128,128]{2,1,0:T(8,128)S(1)}, f32[2,128,128]{2,1,0:T(8,128)S(1)}, u32[]{:S(2)}, u32[]{:S(2)}) collective-permute-start(f32[2,128,128]{2,1,0:T(8,128)S(1)} %get-tuple-element.131.mine), channel_id=1, source_target_pairs={{0,1},{1,0},{2,3},{3,2},{4,5},{5,4},{6,7},{7,6},{8,9},{9,8},{10,11... | collective-permute-start | bytes 393224 | tf_op jit(solution)/shard_map/ppermute | solution.py:551
  101.5 1.6 %collective-permute-start.36 = (f32[2,128,128]{2,1,0:T(8,128)S(1)}, f32[2,128,128]{2,1,0:T(8,128)S(1)}, u32[]{:S(2)}, u32[]{:S(2)}) collective-permute-start(f32[2,128,128]{2,1,0:T(8,128)S(1)} %get-tuple-element.126.mine), channel_id=1, source_target_pairs={{0,1},{1,0},{2,3},{3,2},{4,5},{5,4},{6,7},{7,6},{8,9},{9,8},{10,11... | collective-permute-start | bytes 393224 | tf_op jit(solution)/shard_map/ppermute | solution.py:551
  105.9 1.5 %collective-permute-start.34 = (f32[2,128,128]{2,1,0:T(8,128)S(1)}, f32[2,128,128]{2,1,0:T(8,128)S(1)}, u32[]{:S(2)}, u32[]{:S(2)}) collective-permute-start(f32[2,128,128]{2,1,0:T(8,128)S(1)} %get-tuple-element.122.mine), channel_id=1, source_target_pairs={{0,1},{1,0},{2,3},{3,2},{4,5},{5,4},{6,7},{7,6},{8,9},{9,8},{10,11... | collective-permute-start | bytes 393224 | tf_op jit(solution)/shard_map/ppermute | solution.py:551
  114.1 2.0 %collective-permute-done.34.other = f32[2,128,128]{2,1,0:T(8,128)S(1)} collective-permute-done((f32[2,128,128]{2,1,0:T(8,128)S(1)}, f32[2,128,128]{2,1,0:T(8,128)S(1)}, u32[]{:S(2)}, u32[]{:S(2)}) %collective-permute-start.34) | collective-permute-done | bytes 131104 | tf_op jit(solution)/shard_map/ppermute | solution.py:551
  (111 shorter events, 35.4 us)
Async XLA Ops:
  2.0 15.9 %collective-permute-start.2 = (f32[2,8,16,128]{3,2,1,0:T(8,128)S(1)}, f32[2,8,16,128]{3,2,1,0:T(8,128)S(1)}, u32[]{:S(2)}, u32[]{:S(2)}) collective-permute-start(f32[2,8,16,128]{3,2,1,0:T(8,128)S(1)} %get-tuple-element.155), channel_id=1, source_target_pairs={{0,24},{4,28},{8,16},{12,20},{16,8},{20,12},{24,0},{28,4},{1,25},{... | collective-permute-start | bytes 393224 | tf_op jit(solution)/shard_map/ppermute | solution.py:411
  7.2 11.2 %collective-permute-start.1 = (f32[2,8,16,128]{3,2,1,0:T(8,128)S(1)}, f32[2,8,16,128]{3,2,1,0:T(8,128)S(1)}, u32[]{:S(2)}, u32[]{:S(2)}) collective-permute-start(f32[2,8,16,128]{3,2,1,0:T(8,128)S(1)} %get-tuple-element.155), channel_id=1, source_target_pairs={{0,16},{4,20},{8,24},{12,28},{16,0},{20,4},{24,8},{28,12},{1,17},{... | collective-permute-start | bytes 393224 | tf_op jit(solution)/shard_map/ppermute | solution.py:411
  7.2 11.2 %collective-permute-start = (f32[2,8,16,128]{3,2,1,0:T(8,128)S(1)}, f32[2,8,16,128]{3,2,1,0:T(8,128)S(1)}, u32[]{:S(2)}, u32[]{:S(2)}) collective-permute-start(f32[2,8,16,128]{3,2,1,0:T(8,128)S(1)} %get-tuple-element.155), channel_id=1, source_target_pairs={{0,8},{4,12},{8,0},{12,4},{16,24},{20,28},{24,16},{28,20},{1,9},{5... | collective-permute-start | bytes 393224 | tf_op jit(solution)/shard_map/ppermute | solution.py:411
  8.8 13.2 %collective-permute-start.9 = (f32[2,8,32,128]{3,2,1,0:T(8,128)S(1)}, f32[2,8,32,128]{3,2,1,0:T(8,128)S(1)}, u32[]{:S(2)}, u32[]{:S(2)}) collective-permute-start(f32[2,8,32,128]{3,2,1,0:T(8,128)S(1)} %constant_dynamic-slice_fusion.2), channel_id=1, source_target_pairs={{0,8},{4,12},{8,0},{12,4},{16,24},{20,28},{24,16},{28,20},{1,9},{5... | collective-permute-start | bytes 786440 | tf_op jit(solution)/shard_map/ppermute | solution.py:413
  11.4 14.9 %collective-permute-start.5 = (f32[2,8,64,128]{3,2,1,0:T(8,128)S(1)}, f32[2,8,64,128]{3,2,1,0:T(8,128)S(1)}, u32[]{:S(2)}, u32[]{:S(2)}) collective-permute-start(f32[2,8,64,128]{3,2,1,0:T(8,128)S(1)} %get-tuple-element.157), channel_id=1, source_target_pairs={{0,2},{2,0},{1,3},{3,1},{4,6},{6,4},{5,7},{7,5},{8,10},{10,8},{9,1... | collective-permute-start | bytes 1572872 | tf_op jit(solution)/shard_map/ppermute | solution.py:412
  18.4 14.3 %collective-permute-start.7 = (f32[6,8,16,128]{3,2,1,0:T(8,128)S(1)}, f32[6,8,16,128]{3,2,1,0:T(8,128)S(1)}, u32[]{:S(2)}, u32[]{:S(2)}) collective-permute-start(f32[6,8,16,128]{3,2,1,0:T(8,128)S(1)} %constant_dynamic-update-slice_fusion), channel_id=1, source_target_pairs={{0,2},{2,0},{1,3},{3,1},{4,6},{6,4},{5,7},{7,5},{8,10},{10,8},{9,1... | collective-permute-start | bytes 1179656 | tf_op jit(solution)/shard_map/ppermute | solution.py:444
  20.0 8.4 %collective-permute-start.3 = (f32[6,8,16,128]{3,2,1,0:T(8,128)S(1)}, f32[6,8,16,128]{3,2,1,0:T(8,128)S(1)}, u32[]{:S(2)}, u32[]{:S(2)}) collective-permute-start(f32[6,8,16,128]{3,2,1,0:T(8,128)S(1)} %constant_dynamic-update-slice_fusion), channel_id=1, source_target_pairs={{0,4},{4,0},{8,12},{12,8},{16,20},{20,16},{24,28},{28,24},{1,5},{5... | collective-permute-start | bytes 1179656 | tf_op jit(solution)/shard_map/ppermute | solution.py:443
  22.0 14.6 %collective-permute-start.10 = (f32[4,8,16,128]{3,2,1,0:T(8,128)S(1)}, f32[4,8,16,128]{3,2,1,0:T(8,128)S(1)}, u32[]{:S(2)}, u32[]{:S(2)}) collective-permute-start(f32[4,8,16,128]{3,2,1,0:T(8,128)S(1)} %pad_maximum_fusion.5), channel_id=1, source_target_pairs={{0,16},{4,20},{8,24},{12,28},{16,0},{20,4},{24,8},{28,12},{1,17},{... | collective-permute-start | bytes 786440 | tf_op jit(solution)/shard_map/ppermute | solution.py:424
  26.4 10.9 %collective-permute-start.11 = (f32[4,8,16,128]{3,2,1,0:T(8,128)S(1)}, f32[4,8,16,128]{3,2,1,0:T(8,128)S(1)}, u32[]{:S(2)}, u32[]{:S(2)}) collective-permute-start(f32[4,8,16,128]{3,2,1,0:T(8,128)S(1)} %pad_maximum_fusion.6), channel_id=1, source_target_pairs={{0,8},{4,12},{8,0},{12,4},{16,24},{20,28},{24,16},{28,20},{1,9},{5... | collective-permute-start | bytes 786440 | tf_op jit(solution)/shard_map/ppermute | solution.py:445
  28.4 10.4 %collective-permute-start.4 = (f32[2,8,64,128]{3,2,1,0:T(8,128)S(1)}, f32[2,8,64,128]{3,2,1,0:T(8,128)S(1)}, u32[]{:S(2)}, u32[]{:S(2)}) collective-permute-start(f32[2,8,64,128]{3,2,1,0:T(8,128)S(1)} %get-tuple-element.87), channel_id=1, source_target_pairs={{0,4},{4,0},{8,12},{12,8},{16,20},{20,16},{24,28},{28,24},{1,5},{5... | collective-permute-start | bytes 1572872 | tf_op jit(solution)/shard_map/ppermute | solution.py:448
  28.5 10.8 %collective-permute-start.6 = (f32[2,8,64,128]{3,2,1,0:T(8,128)S(1)}, f32[2,8,64,128]{3,2,1,0:T(8,128)S(1)}, u32[]{:S(2)}, u32[]{:S(2)}) collective-permute-start(f32[2,8,64,128]{3,2,1,0:T(8,128)S(1)} %collective-permute-done.5), channel_id=1, source_target_pairs={{0,4},{4,0},{8,12},{12,8},{16,20},{20,16},{24,28},{28,24},{1,5},{5... | collective-permute-start | bytes 1572872 | tf_op jit(solution)/shard_map/ppermute | solution.py:449
  36.6 13.6 %collective-permute-start.17 = (f32[4,8,16,128]{3,2,1,0:T(8,128)S(1)}, f32[4,8,16,128]{3,2,1,0:T(8,128)S(1)}, u32[]{:S(2)}, u32[]{:S(2)}) collective-permute-start(f32[4,8,16,128]{3,2,1,0:T(8,128)S(1)} %pad_maximum_fusion.7), channel_id=1, source_target_pairs={{0,16},{4,20},{8,24},{12,28},{16,0},{20,4},{24,8},{28,12},{1,17},{... | collective-permute-start | bytes 786440 | tf_op jit(solution)/shard_map/ppermute | solution.py:424
  37.2 13.1 %collective-permute-start.13 = (f32[6,8,16,128]{3,2,1,0:T(8,128)S(1)}, f32[6,8,16,128]{3,2,1,0:T(8,128)S(1)}, u32[]{:S(2)}, u32[]{:S(2)}) collective-permute-start(f32[6,8,16,128]{3,2,1,0:T(8,128)S(1)} %pad_maximum_fusion.3), channel_id=1, source_target_pairs={{0,2},{2,0},{1,3},{3,1},{4,6},{6,4},{5,7},{7,5},{8,10},{10,8},{9,1... | collective-permute-start | bytes 1179656 | tf_op jit(solution)/shard_map/ppermute | solution.py:479
  38.7 12.3 %collective-permute-start.15 = (f32[2,8,16,128]{3,2,1,0:T(8,128)S(1)}, f32[2,8,16,128]{3,2,1,0:T(8,128)S(1)}, u32[]{:S(2)}, u32[]{:S(2)}) collective-permute-start(f32[2,8,16,128]{3,2,1,0:T(8,128)S(1)} %get-tuple-element.165), channel_id=1, source_target_pairs={{0,4},{4,0},{8,12},{12,8},{16,20},{20,16},{24,28},{28,24},{1,5},{5... | collective-permute-start | bytes 393224 | tf_op jit(solution)/shard_map/ppermute | solution.py:470
  38.8 12.3 %collective-permute-start.14 = (f32[2,8,16,128]{3,2,1,0:T(8,128)S(1)}, f32[2,8,16,128]{3,2,1,0:T(8,128)S(1)}, u32[]{:S(2)}, u32[]{:S(2)}) collective-permute-start(f32[2,8,16,128]{3,2,1,0:T(8,128)S(1)} %get-tuple-element.166), channel_id=1, source_target_pairs={{0,4},{4,0},{8,12},{12,8},{16,20},{20,16},{24,28},{28,24},{1,5},{5... | collective-permute-start | bytes 393224 | tf_op jit(solution)/shard_map/ppermute | solution.py:470
  41.6 14.0 %collective-permute-start.21 = (f32[4,16,16,128]{3,2,1,0:T(8,128)S(1)}, f32[4,16,16,128]{3,2,1,0:T(8,128)S(1)}, u32[]{:S(2)}, u32[]{:S(2)}) collective-permute-start(f32[4,16,16,128]{3,2,1,0:T(8,128)S(1)} %get-tuple-element.101), channel_id=1, source_target_pairs={{0,1},{1,0},{2,3},{3,2},{4,5},{5,4},{6,7},{7,6},{8,9},{9,8},{10,11... | collective-permute-start | bytes 1572872 | tf_op jit(solution)/shard_map/ppermute | solution.py:499
  50.3 12.4 %collective-permute-start.25 = (f32[8,8,16,128]{3,2,1,0:T(8,128)S(1)}, f32[8,8,16,128]{3,2,1,0:T(8,128)S(1)}, u32[]{:S(2)}, u32[]{:S(2)}) collective-permute-start(f32[8,8,16,128]{3,2,1,0:T(8,128)S(1)} %pad_maximum_fusion.2), channel_id=1, source_target_pairs={{8,16},{12,20},{16,8},{20,12},{9,17},{13,21},{17,9},{21,13},{10,18... | collective-permute-start | bytes 1572872 | tf_op jit(solution)/shard_map/ppermute | solution.py:434
  51.6 11.1 %collective-permute-start.19 = (f32[6,8,16,128]{3,2,1,0:T(8,128)S(1)}, f32[6,8,16,128]{3,2,1,0:T(8,128)S(1)}, u32[]{:S(2)}, u32[]{:S(2)}) collective-permute-start(f32[6,8,16,128]{3,2,1,0:T(8,128)S(1)} %pad_maximum_fusion.4), channel_id=1, source_target_pairs={{0,2},{2,0},{1,3},{3,1},{4,6},{6,4},{5,7},{7,5},{8,10},{10,8},{9,1... | collective-permute-start | bytes 1179656 | tf_op jit(solution)/shard_map/ppermute | solution.py:479
  55.7 14.0 %collective-permute-start.22 = (f32[4,16,16,128]{3,2,1,0:T(8,128)S(1)}, f32[4,16,16,128]{3,2,1,0:T(8,128)S(1)}, u32[]{:S(2)}, u32[]{:S(2)}) collective-permute-start(f32[4,16,16,128]{3,2,1,0:T(8,128)S(1)} %get-tuple-element.103), channel_id=1, source_target_pairs={{0,1},{1,0},{2,3},{3,2},{4,5},{5,4},{6,7},{7,6},{8,9},{9,8},{10,11... | collective-permute-start | bytes 1572872 | tf_op jit(solution)/shard_map/ppermute | solution.py:499
  62.7 15.0 %collective-permute-start.26 = (f32[8,8,16,128]{3,2,1,0:T(8,128)S(1)}, f32[8,8,16,128]{3,2,1,0:T(8,128)S(1)}, u32[]{:S(2)}, u32[]{:S(2)}) collective-permute-start(f32[8,8,16,128]{3,2,1,0:T(8,128)S(1)} %collective-permute-done.25), channel_id=1, source_target_pairs={{8,0},{12,4},{16,24},{20,28},{9,1},{13,5},{17,25},{21,29},{10,2},{... | collective-permute-start | bytes 1572872 | tf_op jit(solution)/shard_map/ppermute | solution.py:435
  69.7 9.3 %collective-permute-start.23 = (f32[4,8,16,128]{3,2,1,0:T(8,128)S(1)}, f32[4,8,16,128]{3,2,1,0:T(8,128)S(1)}, u32[]{:S(2)}, u32[]{:S(2)}) collective-permute-start(f32[4,8,16,128]{3,2,1,0:T(8,128)S(1)} %get-tuple-element.106), channel_id=1, source_target_pairs={{0,1},{1,0},{2,3},{3,2},{4,5},{5,4},{6,7},{7,6},{8,9},{9,8},{10,11... | collective-permute-start | bytes 786440 | tf_op jit(solution)/shard_map/ppermute | solution.py:499
  81.9 8.6 %collective-permute-start.31 = (f32[4,8,16,128]{3,2,1,0:T(8,128)S(1)}, f32[4,8,16,128]{3,2,1,0:T(8,128)S(1)}, u32[]{:S(2)}, u32[]{:S(2)}) collective-permute-start(f32[4,8,16,128]{3,2,1,0:T(8,128)S(1)} %get-tuple-element.114), channel_id=1, source_target_pairs={{0,2},{2,0},{1,3},{3,1},{4,6},{6,4},{5,7},{7,5},{8,10},{10,8},{9,1... | collective-permute-start | bytes 786440 | tf_op jit(solution)/shard_map/ppermute | solution.py:519
  83.3 16.6 %collective-permute-start.24 = (f32[4,8,16,128]{3,2,1,0:T(8,128)S(1)}, f32[4,8,16,128]{3,2,1,0:T(8,128)S(1)}, u32[]{:S(2)}, u32[]{:S(2)}) collective-permute-start(f32[4,8,16,128]{3,2,1,0:T(8,128)S(1)} %get-tuple-element.107), channel_id=1, source_target_pairs={{0,1},{1,0},{2,3},{3,2},{4,5},{5,4},{6,7},{7,6},{8,9},{9,8},{10,11... | collective-permute-start | bytes 786440 | tf_op jit(solution)/shard_map/ppermute | solution.py:499
  90.5 10.0 %collective-permute-start.32 = (f32[4,8,16,128]{3,2,1,0:T(8,128)S(1)}, f32[4,8,16,128]{3,2,1,0:T(8,128)S(1)}, u32[]{:S(2)}, u32[]{:S(2)}) collective-permute-start(f32[4,8,16,128]{3,2,1,0:T(8,128)S(1)} %get-tuple-element.118), channel_id=1, source_target_pairs={{0,2},{2,0},{1,3},{3,1},{4,6},{6,4},{5,7},{7,5},{8,10},{10,8},{9,1... | collective-permute-start | bytes 786440 | tf_op jit(solution)/shard_map/ppermute | solution.py:519
  92.9 12.4 %collective-permute-start.40 = (f32[2,128,128]{2,1,0:T(8,128)S(1)}, f32[2,128,128]{2,1,0:T(8,128)S(1)}, u32[]{:S(2)}, u32[]{:S(2)}) collective-permute-start(f32[2,128,128]{2,1,0:T(8,128)S(1)} %get-tuple-element.135.mine), channel_id=1, source_target_pairs={{0,1},{1,0},{2,3},{3,2},{4,5},{5,4},{6,7},{7,6},{8,9},{9,8},{10,11... | collective-permute-start | bytes 393224 | tf_op jit(solution)/shard_map/ppermute | solution.py:551
  95.5 10.3 %collective-permute-start.39 = (f32[2,128,128]{2,1,0:T(8,128)S(1)}, f32[2,128,128]{2,1,0:T(8,128)S(1)}, u32[]{:S(2)}, u32[]{:S(2)}) collective-permute-start(f32[2,128,128]{2,1,0:T(8,128)S(1)} %get-tuple-element.133.mine), channel_id=1, source_target_pairs={{0,1},{1,0},{2,3},{3,2},{4,5},{5,4},{6,7},{7,6},{8,9},{9,8},{10,11... | collective-permute-start | bytes 393224 | tf_op jit(solution)/shard_map/ppermute | solution.py:551
  97.2 11.3 %collective-permute-start.38 = (f32[2,128,128]{2,1,0:T(8,128)S(1)}, f32[2,128,128]{2,1,0:T(8,128)S(1)}, u32[]{:S(2)}, u32[]{:S(2)}) collective-permute-start(f32[2,128,128]{2,1,0:T(8,128)S(1)} %get-tuple-element.131.mine), channel_id=1, source_target_pairs={{0,1},{1,0},{2,3},{3,2},{4,5},{5,4},{6,7},{7,6},{8,9},{9,8},{10,11... | collective-permute-start | bytes 393224 | tf_op jit(solution)/shard_map/ppermute | solution.py:551
  99.9 11.6 %collective-permute-start.37 = (f32[2,128,128]{2,1,0:T(8,128)S(1)}, f32[2,128,128]{2,1,0:T(8,128)S(1)}, u32[]{:S(2)}, u32[]{:S(2)}) collective-permute-start(f32[2,128,128]{2,1,0:T(8,128)S(1)} %get-tuple-element.129.mine), channel_id=1, source_target_pairs={{0,1},{1,0},{2,3},{3,2},{4,5},{5,4},{6,7},{7,6},{8,9},{9,8},{10,11... | collective-permute-start | bytes 393224 | tf_op jit(solution)/shard_map/ppermute | solution.py:551
  101.5 10.8 %collective-permute-start.36 = (f32[2,128,128]{2,1,0:T(8,128)S(1)}, f32[2,128,128]{2,1,0:T(8,128)S(1)}, u32[]{:S(2)}, u32[]{:S(2)}) collective-permute-start(f32[2,128,128]{2,1,0:T(8,128)S(1)} %get-tuple-element.126.mine), channel_id=1, source_target_pairs={{0,1},{1,0},{2,3},{3,2},{4,5},{5,4},{6,7},{7,6},{8,9},{9,8},{10,11... | collective-permute-start | bytes 393224 | tf_op jit(solution)/shard_map/ppermute | solution.py:551
  105.3 8.0 %collective-permute-start.35 = (f32[2,128,128]{2,1,0:T(8,128)S(1)}, f32[2,128,128]{2,1,0:T(8,128)S(1)}, u32[]{:S(2)}, u32[]{:S(2)}) collective-permute-start(f32[2,128,128]{2,1,0:T(8,128)S(1)} %get-tuple-element.124.mine), channel_id=1, source_target_pairs={{0,1},{1,0},{2,3},{3,2},{4,5},{5,4},{6,7},{7,6},{8,9},{9,8},{10,11... | collective-permute-start | bytes 393224 | tf_op jit(solution)/shard_map/ppermute | solution.py:551
  105.9 10.2 %collective-permute-start.34 = (f32[2,128,128]{2,1,0:T(8,128)S(1)}, f32[2,128,128]{2,1,0:T(8,128)S(1)}, u32[]{:S(2)}, u32[]{:S(2)}) collective-permute-start(f32[2,128,128]{2,1,0:T(8,128)S(1)} %get-tuple-element.122.mine), channel_id=1, source_target_pairs={{0,1},{1,0},{2,3},{3,2},{4,5},{5,4},{6,7},{7,6},{8,9},{9,8},{10,11... | collective-permute-start | bytes 393224 | tf_op jit(solution)/shard_map/ppermute | solution.py:551
  108.5 9.1 %collective-permute-start.33 = (f32[2,128,128]{2,1,0:T(8,128)S(1)}, f32[2,128,128]{2,1,0:T(8,128)S(1)}, u32[]{:S(2)}, u32[]{:S(2)}) collective-permute-start(f32[2,128,128]{2,1,0:T(8,128)S(1)} %get-tuple-element.120.mine), channel_id=1, source_target_pairs={{0,1},{1,0},{2,3},{3,2},{4,5},{5,4},{6,7},{7,6},{8,9},{9,8},{10,11... | collective-permute-start | bytes 393224 | tf_op jit(solution)/shard_map/ppermute | solution.py:551
  (16 other events, 89.6 us)
